TPU v7x, 256 devices: a whole 4x4x8 slice. The times are simulated.
256 devices in a mesh: band: 16 (over z, core), grid: 16 (over y, x).
Axes of the slice: x: 4, y: 4, z: 8, core: 2. Of those that a mesh axis runs over, the one named last changes fastest.
Arguments:
- psi: bfloat16 [128, 3145728], P('grid', 'band'), may hold values from -6 to 6
- tiles: bfloat16 [24576, 2, 128, 64], P(('band', 'grid')), may hold values from -0.5 to 0.5
- tile_block: int32 [24576, 2], P(('band', 'grid')), may hold values from 0 to 31, as said below
- couplings: float32 [2, 16, 16], replicated, as said below
- species: int32 [128], P('band'), may hold values from 0 to 1
Outputs:
- applied: bfloat16 [128, 3145728], P('grid', 'band')
Inputs may be any that keep to these rules, and one draw needn't show every extreme that they name: `tile_block`: row r lies in slab s = r // 1536; its tiles name blocks s * 2 to (s + 1) * 2 - 1, or, for s > 0, one of the last 1 block of slab s - 1, s * 2 - 1 to s * 2 - 1. `couplings`: each species' matrix is symmetric.
All inputs are finite; a program needn't handle non-finite values.
Results may differ from a plain program's by a relative error of at most 0.0095.
Values may be sent and summed in bfloat16 or wider, within the bound.
No kernel may reach another device: no remote copies, remote signals or barrier semaphores. Data moves between devices by JAX's collectives and lax.ppermute only.
A program may use at most 64 MiB of HBM per device.

v0:
```python
import jax
import jax.numpy as jnp
from jax import lax
from jax.sharding import PartitionSpec as P

BLK = 2
EDGE = 1


def from_behind(block, axis, distance):
    devices = range(lax.axis_size(axis))
    route = [(i - distance, i) for i in devices if i - distance in devices]
    return lax.ppermute(block, axis, route)


def couple(blocks, kinds, couplings):
    count, width, depth = blocks.shape
    atom_proj = couplings.shape[1]
    per_atom = blocks.reshape(count * (width // atom_proj), atom_proj, depth)
    table = jnp.zeros((per_atom.shape[0], atom_proj, atom_proj), jnp.float32)
    for kind in range(couplings.shape[0]):
        table = table + jnp.where((kinds == kind)[:, None, None], couplings[kind], jnp.float32(0.0))
    mixed = jnp.einsum("aij,ajn->ain", table, per_atom, precision=lax.Precision.HIGHEST)
    return mixed.reshape(count, width, depth)


def body(psi, tiles, tile_block, couplings, species):
    splits = lax.axis_size("grid")
    local_bands, slab_points = psi.shape
    rows, per_row, tile, proj = tiles.shape
    bands = local_bands * splits
    spread = lax.all_to_all(
        psi.reshape(local_bands, splits, rows * tile),
        "grid",
        split_axis=1,
        concat_axis=0,
        tiled=True,
    )
    columns = spread.reshape(bands, rows, tile)
    partial_value = jnp.einsum("rjip,nri->rjpn", tiles, columns, preferred_element_type=jnp.float32)
    slab = lax.axis_index("band")
    local_ids = tile_block - (slab * BLK - EDGE)
    slots = BLK + EDGE
    onehot = (local_ids.reshape(-1)[None, :] == jnp.arange(slots, dtype=jnp.int32)[:, None]).astype(
        jnp.float32
    )
    summed = jnp.dot(
        onehot,
        partial_value.reshape(rows * per_row, proj * bands),
        precision=lax.Precision.HIGH,
        preferred_element_type=jnp.float32,
    ).reshape(slots, proj, bands)
    own, edge = lax.psum((summed[EDGE:], summed[:EDGE]), "grid")
    later = from_behind(edge.astype(jnp.bfloat16), "band", -1).astype(edge.dtype)
    own = jnp.concatenate([own[: BLK - EDGE], own[BLK - EDGE :] + later], axis=0)
    coupled = couple(own, species, couplings).astype(jnp.bfloat16)
    earlier = from_behind(coupled[BLK - EDGE :], "band", 1)
    table = jnp.concatenate([earlier, coupled], axis=0)
    picked = jnp.take(table, local_ids, axis=0)
    result = jnp.einsum("rjip,rjpn->nri", tiles, picked, preferred_element_type=jnp.float32).astype(
        jnp.bfloat16
    )
    returned = lax.all_to_all(
        result.reshape(bands, 1, rows * tile), "grid", split_axis=0, concat_axis=1, tiled=True
    )
    return returned.reshape(local_bands, slab_points)


def solution(mesh):
    return jax.shard_map(
        body,
        mesh=mesh,
        in_specs=(
            P("grid", "band"),
            P(("band", "grid"), None, None, None),
            P(("band", "grid"), None),
            P(),
            P("band"),
        ),
        out_specs=P("grid", "band"),
        check_vma=False,
    )
```

profile of v0, /device:TPU:97, one launch (start us, length us, event | category | flops | bytes accessed | tf_op | source)
XLA Modules:
  0.0 264.9 jit_solution(15208685479456181829)
XLA Ops:
  6.5 0.0 copy-start
  6.5 7.1 %all-to-all-start = ((bf16[8,16,12288]{2,0,1:T(8,128)(2,1)}), bf16[8,16,12288]{2,0,1:T(8,128)(2,1)}, u32[]{:S(2)}, u32[]{:S(2)}) async-start(bf16[8,16,12288]{2,0,1:T(8,128)(2,1)} %bitcast.48), calls=%async_computation | async-start | bytes 6291456 | tf_op jit(solution)/shard_map/all_to_all | solution.py:32
  13.6 0.0 all-reduce.2.cloned.1.call-start
  13.7 0.1 copy.14
  13.8 0.1 eq.23
  14.0 46.3 %all-to-all-done = bf16[8,16,12288]{2,0,1:T(8,128)(2,1)} async-done(((bf16[8,16,12288]{2,0,1:T(8,128)(2,1)}), bf16[8,16,12288]{2,0,1:T(8,128)(2,1)}, u32[]{:S(2)}, u32[]{:S(2)}) %all-to-all-start) | async-done | bytes 3145760 | tf_op jit(solution)/shard_map/all_to_all | solution.py:32
  60.3 2.6 copy.23
  62.9 2.3 fusion.3
  65.2 0.0 copy-start.3
  65.2 4.5 %fusion = f32[3,8192]{1,0:T(4,128)S(1)} fusion(f32[24,8,64,128]{3,2,1,0:T(8,128)S(1)} %bitcast.44, s32[192]{0:T(256)S(1)} %eq.23), kind=kOutput, calls=%fused_computation.1 | convolution fusion | flops 28312128 | bytes 6390528 | tf_op jit(solution)/shard_map/dot_general | solution.py:47
  69.8 0.6 copy.33
  70.5 0.0 all-reduce.2.cloned.1.call-update
  70.5 56.8 %psum.15 = bf16[1,64,128]{2,1,0:T(8,128)(2,1)S(1)} all-reduce(f32[1,64,128]{2,1,0:T(8,128)S(1)} %bitcast.52), channel_id=1, replica_groups=mesh['band'=16,'grid'=16] {'grid'}, use_global_device_ids=true, to_apply=%region_1.0 | all-reduce | flops 8192 | bytes 49152 | tf_op jit(solution)/shard_map/psum | solution.py:53
  127.3 17.8 %collective-permute-start = (bf16[1,64,128]{2,1,0:T(8,128)(2,1)S(1)}, bf16[1,64,128]{2,1,0:T(8,128)(2,1)S(1)}, u32[]{:S(2)}, u32[]{:S(2)}) collective-permute-start(bf16[1,64,128]{2,1,0:T(8,128)(2,1)S(1)} %psum.15), channel_id=1, source_target_pairs={{16,0},{32,16},{48,32},{64,48},{80,64},{96,80},{112,96},{128,112},... | collective-permute-start | bytes 49160 | tf_op jit(solution)/shard_map/ppermute | solution.py:13
  145.1 0.1 copy.16
  145.2 0.1 reshape.42
  145.3 3.9 %collective-permute-done = bf16[1,64,128]{2,1,0:T(8,128)(2,1)S(1)} collective-permute-done((bf16[1,64,128]{2,1,0:T(8,128)(2,1)S(1)}, bf16[1,64,128]{2,1,0:T(8,128)(2,1)S(1)}, u32[]{:S(2)}, u32[]{:S(2)}) %collective-permute-start) | collective-permute-done | bytes 16416 | tf_op jit(solution)/shard_map/ppermute | solution.py:13
  149.2 11.3 %all-reduce.2.cloned.1.call-done = f32[2,64,128]{2,1,0:T(8,128)} async-done(((f32[2,64,128]{2,1,0:T(8,128)}), f32[2,64,128]{2,1,0:T(8,128)}) %all-reduce.2.cloned.1.call-update) | async-done | bytes 65552 | tf_op jit(solution)/shard_map/psum | solution.py:53
  160.5 0.8 fusion.22
  161.3 0.3 convolution_convert_fusion
  161.6 6.7 %collective-permute-start.1 = (bf16[1,64,128]{2,1,0:T(8,128)(2,1)S(1)}, bf16[1,64,128]{2,1,0:T(8,128)(2,1)S(1)}, u32[]{:S(2)}, u32[]{:S(2)}) collective-permute-start(bf16[1,64,128]{2,1,0:T(8,128)(2,1)S(1)} %bitcast.53), channel_id=1, source_target_pairs={{0,16},{16,32},{32,48},{48,64},{64,80},{80,96},{96,112},{112,128},... | collective-permute-start | bytes 49160 | tf_op jit(solution)/shard_map/ppermute | solution.py:13
  168.3 0.1 copy.13
  168.4 0.5 collective-permute-done.1
  168.9 2.7 %gather_fusion = bf16[192,64,128]{2,1,0:T(8,128)(2,1)} fusion(bf16[3,64,128]{2,1,0:T(8,128)(2,1)S(1)} %pad_maximum_fusion.1, s32[1024]{0:T(1024)S(1)} %pad_clamp_fusion), kind=kCustom, calls=%fused_computation | custom fusion | bytes 6292224 | tf_op jit(solution)/shard_map/jit(_take)/gather | solution.py:59
  171.7 5.0 %bitcast_convert_fusion = bf16[96,128,128]{1,2,0:T(8,128)(2,1)} fusion(bf16[96,2,128,64]{2,3,1,0:T(8,128)(2,1)S(1)} %copy-done, bf16[96,2,64,128]{3,2,1,0:T(8,128)(2,1)} %bitcast.46, pred[96,2]{1,0:T(8,128)(4,1)S(1)} %copy.13), kind=kOutput, calls=%fused_computation.4 | convolution fusion | flops 405798912 | bytes 9437376 | tf_op jit(solution)/shard_map/rjip,rjpn->nri/dot_general | solution.py:60
  176.6 0.5 broadcast.19
  177.1 5.2 %reduce = bf16[128,12288]{0,1:T(8,128)(2,1)} reduce(bf16[128,1,12288]{0,2,1:T(8,128)(2,1)} %bitcast.45, bf16[]{:T(256)} %broadcast.19), dimensions={1}, to_apply=%copy.17.reduce_sub_computation | reduce | bytes 6291458 | tf_op jit(solution)/shard_map/reshape | solution.py:64
  182.3 4.7 %copy.34 = bf16[128,12288]{1,0:T(8,128)(2,1)} copy(bf16[128,12288]{0,1:T(8,128)(2,1)} %reduce) | data formatting | bytes 6291456
  187.0 7.5 %reshape.52 = bf16[16,2,49152]{2,1,0:T(2,128)(2,1)} reshape(bf16[128,12288]{1,0:T(8,128)(2,1)} %copy.34) | data formatting | bytes 6291456
  194.5 44.3 %all_to_all.30 = bf16[16,2,49152]{2,1,0:T(2,128)(2,1)} all-to-all(bf16[16,2,49152]{2,1,0:T(2,128)(2,1)} %reshape.52), channel_id=1, replica_groups=mesh['band'=16,'grid'=16] {'grid'}, dimensions={0} | all-to-all | bytes 6291456 | tf_op jit(solution)/shard_map/all_to_all | solution.py:63
  238.8 11.5 %reshape.53 = bf16[128,1,12288]{2,1,0:T(2,128)(2,1)} reshape(bf16[16,2,49152]{2,1,0:T(2,128)(2,1)} %all_to_all.30) | data formatting | bytes 6291456
  250.3 7.8 %copy.22 = bf16[128,1,12288]{2,0,1:T(8,128)(2,1)} copy(bf16[128,1,12288]{2,1,0:T(2,128)(2,1)} %reshape.53) | data formatting | bytes 6291456
  (16 shorter events, 0.1 us)
Async XLA Ops:
  6.5 56.4 %copy-start = (bf16[96,2,128,64]{2,3,1,0:T(8,128)(2,1)S(1)}, bf16[96,2,128,64]{2,3,1,0:T(8,128)(2,1)}, u32[]{:S(2)}) copy-start(bf16[96,2,128,64]{2,3,1,0:T(8,128)(2,1)} %param.6) | copy-start | bytes 9437188
  6.5 7.1 %copy-start.2 = (s32[96,2]{0,1:T(2,128)S(1)}, s32[96,2]{0,1:T(2,128)}, u32[]{:S(2)}) copy-start(s32[96,2]{0,1:T(2,128)} %param.7) | copy-start | bytes 2308
  6.5 7.4 %copy-start.1 = (f32[2,16,16]{2,1,0:T(8,128)S(1)}, f32[2,16,16]{2,1,0:T(8,128)}, u32[]{:S(2)}) copy-start(f32[2,16,16]{2,1,0:T(8,128)} %param.8) | copy-start | bytes 6148
  6.5 53.8 %all-to-all-start = ((bf16[8,16,12288]{2,0,1:T(8,128)(2,1)}), bf16[8,16,12288]{2,0,1:T(8,128)(2,1)}, u32[]{:S(2)}, u32[]{:S(2)}) async-start(bf16[8,16,12288]{2,0,1:T(8,128)(2,1)} %bitcast.48), calls=%async_computation | async-start | bytes 6291456 | tf_op jit(solution)/shard_map/all_to_all | solution.py:32
  13.6 146.9 %all-reduce.2.cloned.1.call-start = ((), (), s32[]{:S(2)}) async-start(), calls=%async_computation.2 | async-start | bytes 131072 | tf_op jit(solution)/shard_map/psum | solution.py:53
  65.2 79.8 %copy-start.3 = (s32[8]{0:T(128)S(1)}, s32[8]{0:T(128)}, u32[]{:S(2)}) copy-start(s32[8]{0:T(128)} %param.9) | copy-start | bytes 100
  127.3 21.9 %collective-permute-start = (bf16[1,64,128]{2,1,0:T(8,128)(2,1)S(1)}, bf16[1,64,128]{2,1,0:T(8,128)(2,1)S(1)}, u32[]{:S(2)}, u32[]{:S(2)}) collective-permute-start(bf16[1,64,128]{2,1,0:T(8,128)(2,1)S(1)} %psum.15), channel_id=1, source_target_pairs={{16,0},{32,16},{48,32},{64,48},{80,64},{96,80},{112,96},{128,112},... | collective-permute-start | bytes 49160 | tf_op jit(solution)/shard_map/ppermute | solution.py:13
  161.6 7.4 %collective-permute-start.1 = (bf16[1,64,128]{2,1,0:T(8,128)(2,1)S(1)}, bf16[1,64,128]{2,1,0:T(8,128)(2,1)S(1)}, u32[]{:S(2)}, u32[]{:S(2)}) collective-permute-start(bf16[1,64,128]{2,1,0:T(8,128)(2,1)S(1)} %bitcast.53), channel_id=1, source_target_pairs={{0,16},{16,32},{32,48},{48,64},{64,80},{80,96},{96,112},{112,128},... | collective-permute-start | bytes 49160 | tf_op jit(solution)/shard_map/ppermute | solution.py:13
Sparse Core Ops, SparseCore 0:
  70.6 89.8 all-reduce.1
where the time goes:
time: 267 us; the launch traced here: 265 us
  blocking collectives  101 us (38%)
  waiting for transfers between devices  62 us (23%)
  local copies, waits for them, and re-layouts  38.7 us (14%)
  starting transfers between devices  31.5 us (12%)
  between operations  13.6 us (5%)
  matrix products  12.1 us (5%)
  other arithmetic  6 us (2%)
    psum x1, blocking collectives, body(): own, edge = lax.psum((summed[EDGE:], summed[:EDGE]), 'grid')  56.8 us
    all_to_all x1, waiting for transfers between devices, body(): lax.all_to_all(psi.reshape(local_bands, splits, rows * tile), 'grid', spl...  46.3 us
    all_to_all x1, blocking collectives, body(): lax.all_to_all(result.reshape(bands, 1, rows * tile), 'grid', split_axis=...  44.3 us
    unnamed x15, local copies, waits for them, and re-layouts  34.8 us
    ppermute x2, starting transfers between devices, from_behind(): return lax.ppermute(block, axis, route)  24.4 us
    psum x1, waiting for transfers between devices, body(): own, edge = lax.psum((summed[EDGE:], summed[:EDGE]), 'grid')  11.3 us
    all_to_all x1, starting transfers between devices, body(): lax.all_to_all(psi.reshape(local_bands, splits, rows * tile), 'grid', spl...  7.06 us
  transfers between devices with their start and end apart: 4, of which 4 were waited for; matrix products, arithmetic and copies ran while one was open for 0% of the time, Pallas kernels for 0%

commit v1 on v0

v1 whole, which is shorter than its diff:
```python
import jax
import jax.numpy as jnp
from jax import lax
from jax.experimental import pallas as pl
from jax.experimental.pallas import tpu as pltpu
from jax.sharding import PartitionSpec as P

BLK = 2
EDGE = 1
SLOTS = BLK + EDGE
VMEM_LIMIT = 48 * 1024 * 1024


def whole(space=pltpu.VMEM):
    return pl.BlockSpec(memory_space=space)


def call(kernel, out_shape, in_spaces, out_spaces, scratch=(), flops=0, moved=0):
    single = not isinstance(out_shape, (tuple, list))
    return pl.pallas_call(
        kernel,
        out_shape=out_shape,
        in_specs=[whole(s) for s in in_spaces],
        out_specs=whole(out_spaces) if single else [whole(s) for s in out_spaces],
        scratch_shapes=list(scratch),
        compiler_params=pltpu.CompilerParams(vmem_limit_bytes=VMEM_LIMIT),
        cost_estimate=pl.CostEstimate(flops=flops, bytes_accessed=moved, transcendentals=0),
    )


def forward_kernel(slots_ref, columns_ref, tiles_ref, own_ref, edge_ref, total):
    rows, per_row, proj, tile = tiles_ref.shape
    groups, local, _ = columns_ref.shape
    bands = groups * local
    total[...] = jnp.zeros_like(total)

    def row(r, carry):
        at = pl.ds(pl.multiple_of(r * tile, tile), tile)
        columns = columns_ref[:, :, at].reshape(bands, tile)
        values = tiles_ref[r].reshape(per_row * proj, tile)
        part = lax.dot_general(
            values, columns, (((1,), (1,)), ((), ())), preferred_element_type=jnp.float32
        )
        for j in range(per_row):
            total[slots_ref[r, j]] += part[j * proj : (j + 1) * proj]
        return carry

    lax.fori_loop(0, rows, row, 0, unroll=8)
    own_ref[...] = total[EDGE:].reshape(own_ref.shape)
    edge_ref[...] = total[0].astype(edge_ref.dtype)


def couple_kernel(parts_ref, mix_ref, coupled_ref):
    count = parts_ref.shape[0]
    summed = parts_ref[0].astype(jnp.float32)
    for source in range(1, count):
        summed = summed + parts_ref[source].astype(jnp.float32)
    coupled_ref[...] = jnp.dot(
        mix_ref[...], summed, precision=lax.Precision.HIGHEST, preferred_element_type=jnp.float32
    ).astype(coupled_ref.dtype)


def backward_kernel(slots_ref, earlier_ref, coupled_ref, tiles_ref, out_ref, pairs):
    rows, per_row, proj, tile = tiles_ref.shape
    groups, local, _ = out_ref.shape
    blocks = [earlier_ref[...]] + [coupled_ref[k * proj : (k + 1) * proj] for k in range(BLK)]
    blocks = [b.astype(jnp.float32) for b in blocks]
    for first in range(SLOTS):
        for second in range(SLOTS):
            both = jnp.concatenate([blocks[first], blocks[second]], axis=0)
            pairs[first * SLOTS + second] = both.T.astype(pairs.dtype)

    def row(r, carry):
        at = pl.ds(pl.multiple_of(r * tile, tile), tile)
        values = tiles_ref[r].reshape(per_row * proj, tile)
        chosen = pairs[slots_ref[r, 0] * SLOTS + slots_ref[r, 1]]
        result = jnp.dot(chosen, values, preferred_element_type=jnp.float32)
        out_ref[:, :, at] = result.astype(out_ref.dtype).reshape(groups, local, tile)
        return carry

    lax.fori_loop(0, rows, row, 0, unroll=8)


def from_behind(block, axis, distance):
    devices = range(lax.axis_size(axis))
    route = [(i - distance, i) for i in devices if i - distance in devices]
    return lax.ppermute(block, axis, route)


def mixing(kinds, couplings):
    atoms, width = kinds.shape[0], couplings.shape[1]
    table = jnp.zeros((atoms, width, width), jnp.float32)
    for kind in range(couplings.shape[0]):
        table = table + jnp.where((kinds == kind)[:, None, None], couplings[kind], jnp.float32(0.0))
    same = jnp.eye(atoms, dtype=jnp.bool_)[:, None, :, None]
    spread = jnp.where(same, table[:, :, None, :], jnp.float32(0.0))
    return spread.reshape(atoms * width, atoms * width)


def body(psi, tiles, tile_block, couplings, species):
    splits = lax.axis_size("grid")
    local_bands, slab_points = psi.shape
    rows, per_row, tile, proj = tiles.shape
    bands = local_bands * splits
    points = rows * tile
    flops = 2 * rows * per_row * proj * tile * bands
    moved = 2 * (bands * points + tiles.size)
    slab = lax.axis_index("band")
    slots = tile_block - (slab * BLK - EDGE)
    mix = mixing(species, couplings)
    values = jnp.transpose(tiles, (0, 1, 3, 2))

    spread = lax.all_to_all(
        psi.reshape(local_bands, splits, points), "grid", split_axis=1, concat_axis=0, tiled=True
    ).reshape(splits, local_bands, points)
    own, edge = call(
        forward_kernel,
        (
            jax.ShapeDtypeStruct((BLK * proj, bands), jnp.float32),
            jax.ShapeDtypeStruct((proj, bands), jnp.bfloat16),
        ),
        (pltpu.SMEM, pltpu.VMEM, pltpu.VMEM),
        (pltpu.VMEM, pltpu.VMEM),
        [pltpu.VMEM((SLOTS, proj, bands), jnp.float32)],
        flops,
        moved,
    )(slots, spread, values)
    later = from_behind(edge, "band", -1).astype(jnp.float32)
    last = (BLK - EDGE) * proj
    own = jnp.concatenate([own[:last], own[last:] + later], axis=0).astype(jnp.bfloat16)
    parts = lax.all_to_all(
        jnp.broadcast_to(own[None], (splits,) + own.shape), "grid", 0, 0, tiled=True
    )
    coupled = call(
        couple_kernel,
        jax.ShapeDtypeStruct((BLK * proj, bands), jnp.bfloat16),
        (pltpu.VMEM, pltpu.VMEM),
        pltpu.VMEM,
    )(parts, mix)
    earlier = from_behind(coupled[last:], "band", 1)
    result = call(
        backward_kernel,
        jax.ShapeDtypeStruct((splits, local_bands, points), jnp.bfloat16),
        (pltpu.SMEM, pltpu.VMEM, pltpu.VMEM, pltpu.VMEM),
        pltpu.VMEM,
        [pltpu.VMEM((SLOTS * SLOTS, bands, per_row * proj), jnp.bfloat16)],
        flops,
        moved,
    )(slots, earlier, coupled, values)
    returned = lax.all_to_all(result, "grid", split_axis=0, concat_axis=0, tiled=True)
    return jnp.transpose(returned, (1, 0, 2)).reshape(local_bands, slab_points)


def solution(mesh):
    return jax.shard_map(
        body,
        mesh=mesh,
        in_specs=(
            P("grid", "band"),
            P(("band", "grid"), None, None, None),
            P(("band", "grid"), None),
            P(),
            P("band"),
        ),
        out_specs=P("grid", "band"),
        check_vma=False,
    )
```

time: 267 us -> 137 us (0.51)
  blocking collectives: 101 us -> 41 us
  local copies, waits for them, and re-layouts: 38.7 us -> 2.87 us
  between operations: 13.6 us -> 0.16 us
  matrix products: 12.1 us -> 0 us
  starting transfers between devices: 31.5 us -> 20.2 us
  Pallas kernels: 0 us -> 10.8 us
  other arithmetic: 6 us -> 0.23 us
    psum x1 -> x0, blocking collectives: 56.8 us -> none  [body(): own, edge = lax.psum((summed[EDGE:], summed[:EDGE]), 'grid')]
    unnamed x15 -> x8, local copies, waits for them, and re-layouts: 34.8 us -> 1.78 us
    ppermute x2, starting transfers between devices: 24.4 us -> 9.21 us  [from_behind(): return lax.ppermute(block, axis, route)]
    dot_general x4 -> x0, matrix products: 12.1 us -> none  [the longest x1 4.95 us: body(): jnp.einsum('rjip,rjpn->nri', tiles, picked, preferred_element_type=jnp.fl...]
    psum x1 -> x0, waiting for transfers between devices: 11.3 us -> none  [body(): own, edge = lax.psum((summed[EDGE:], summed[:EDGE]), 'grid')]
    pallas_call x0 -> x3, Pallas kernels: none -> 10.8 us  [the longest x1 5.79 us: body(): call(forward_kernel, (jax.ShapeDtypeStruct((BLK * proj, bands), jnp.float...]
    all_to_all x1 -> x2, waiting for transfers between devices: 46.3 us -> 55.9 us  [the longest x1 46.5 us: body(): lax.all_to_all(psi.reshape(local_bands, splits, points), 'grid', split_ax...]
    reshape x1 -> x0, other arithmetic: 5.18 us -> none  [body(): result.reshape(bands, 1, rows * tile)]
where the time goes in v1:
time: 137 us; the launch traced here: 136 us
  waiting for transfers between devices  60.8 us (44%)
  blocking collectives  41 us (30%)
  starting transfers between devices  20.2 us (15%)
  Pallas kernels  10.8 us (8%)
  local copies, waits for them, and re-layouts  2.87 us (2%)
    all_to_all x1, waiting for transfers between devices, body(): lax.all_to_all(psi.reshape(local_bands, splits, points), 'grid', split_ax...  46.5 us
    all_to_all x1, blocking collectives, body(): lax.all_to_all(result, 'grid', split_axis=0, concat_axis=0, tiled=True)  41 us
    all_to_all x1, waiting for transfers between devices, body(): lax.all_to_all(jnp.broadcast_to(own[None], (splits,) + own.shape), 'grid'...  9.4 us
    ppermute x2, starting transfers between devices, from_behind(): return lax.ppermute(block, axis, route)  9.21 us
    all_to_all x1, starting transfers between devices, body(): lax.all_to_all(psi.reshape(local_bands, splits, points), 'grid', split_ax...  6.89 us
    pallas_call x1, Pallas kernels, body(): call(forward_kernel, (jax.ShapeDtypeStruct((BLK * proj, bands), jnp.float...  5.79 us
    ppermute x2, waiting for transfers between devices, from_behind(): return lax.ppermute(block, axis, route)  4.96 us
    pallas_call x1, Pallas kernels, body(): call(backward_kernel, jax.ShapeDtypeStruct((splits, local_bands, points),...  4.77 us
  transfers between devices with their start and end apart: 4, of which 4 were waited for; matrix products, arithmetic and copies ran while one was open for 0% of the time, Pallas kernels for 0%

profile of v1, /device:TPU:97, one launch (start us, length us, event | category | flops | bytes accessed | tf_op | source)
XLA Modules:
  0.0 136.1 jit_solution(17709147719885737788)
XLA Ops:
  0.0 0.0 copy-start.1
  0.0 0.0 copy-start
  0.0 6.9 %all-to-all-start = ((bf16[8,16,12288]{2,0,1:T(8,128)(2,1)}), bf16[8,16,12288]{2,0,1:T(8,128)(2,1)S(1)}, u32[]{:S(2)}, u32[]{:S(2)}) async-start(bf16[8,16,12288]{2,0,1:T(8,128)(2,1)} %bitcast.20), calls=%async_computation | async-start | bytes 6291456 | tf_op jit(solution)/shard_map/all_to_all | solution.py:113
  6.9 0.0 copy-done.1
  6.9 0.1 copy.6
  7.0 0.0 copy-done
  7.1 46.5 %all-to-all-done = bf16[8,16,12288]{2,0,1:T(8,128)(2,1)S(1)} async-done(((bf16[8,16,12288]{2,0,1:T(8,128)(2,1)}), bf16[8,16,12288]{2,0,1:T(8,128)(2,1)S(1)}, u32[]{:S(2)}, u32[]{:S(2)}) %all-to-all-start) | async-done | bytes 3145760 | tf_op jit(solution)/shard_map/all_to_all | solution.py:113
  53.5 0.0 copy-start.2
  53.5 5.8 %shard_map.55 = (f32[128,128]{1,0:T(8,128)S(1)}, bf16[64,128]{1,0:T(8,128)(2,1)S(1)}) custom-call(s32[96,2]{1,0:T(8,128)S(1)} %broadcast_subtract_fusion.slots_ref, bf16[16,8,12288]{2,1,0:T(8,128)(2,1)S(1)} %bitcast.16, bf16[96,2,64,128]{3,2,1,0:T(8,128)(2,1)} %bitcast.17), custom_call_target="tpu_custom_call" | custom-call | flops 402653184 | bytes 6291456 | tf_op jit(solution)/shard_map/pallas_call | solution.py:116
  59.3 3.7 %collective-permute-start = (bf16[64,128]{1,0:T(8,128)(2,1)S(1)}, bf16[64,128]{1,0:T(8,128)(2,1)S(1)}, u32[]{:S(2)}, u32[]{:S(2)}) collective-permute-start(bf16[64,128]{1,0:T(8,128)(2,1)S(1)} %get-tuple-element.8), channel_id=1, source_target_pairs={{16,0},{32,16},{48,32},{64,48},{80,64},{96,80},{112,96},{128,112},... | collective-permute-start | bytes 49160 | tf_op jit(solution)/shard_map/ppermute | solution.py:87
  63.0 0.0 copy-done.2
  63.1 4.1 %collective-permute-done = bf16[64,128]{1,0:T(8,128)(2,1)S(1)} collective-permute-done((bf16[64,128]{1,0:T(8,128)(2,1)S(1)}, bf16[64,128]{1,0:T(8,128)(2,1)S(1)}, u32[]{:S(2)}, u32[]{:S(2)}) %collective-permute-start) | collective-permute-done | bytes 16416 | tf_op jit(solution)/shard_map/ppermute | solution.py:87
  67.2 0.9 broadcast_in_dim.55
  68.1 4.1 %all-to-all-start.1 = ((bf16[16,128,128]{2,1,0:T(8,128)(2,1)}), bf16[16,128,128]{2,1,0:T(8,128)(2,1)S(1)}, u32[]{:S(2)}, u32[]{:S(2)}) async-start(bf16[16,128,128]{2,1,0:T(8,128)(2,1)} %broadcast_in_dim.55), calls=%async_computation.1 | async-start | bytes 1048576 | tf_op jit(solution)/shard_map/all_to_all | solution.py:131
  72.2 0.1 select_add_fusion
  72.3 0.1 broadcast_select_fusion
  72.4 0.2 select_n.26.mix_ref
  72.6 9.4 %all-to-all-done.1.parts_ref = bf16[16,128,128]{2,1,0:T(8,128)(2,1)S(1)} async-done(((bf16[16,128,128]{2,1,0:T(8,128)(2,1)}), bf16[16,128,128]{2,1,0:T(8,128)(2,1)S(1)}, u32[]{:S(2)}, u32[]{:S(2)}) %all-to-all-start.1) | async-done | bytes 524320 | tf_op jit(solution)/shard_map/all_to_all | solution.py:131
  82.0 0.3 shard_map.56.coupled_ref
  82.3 5.5 %collective-permute-start.1 = (bf16[64,128]{1,0:T(8,128)(2,1)S(1)}, bf16[64,128]{1,0:T(8,128)(2,1)S(1)}, u32[]{:S(2)}, u32[]{:S(2)}) collective-permute-start(bf16[64,128]{1,0:T(8,128)(2,1)S(1)} %slice.22), channel_id=1, source_target_pairs={{0,16},{16,32},{32,48},{48,64},{64,80},{80,96},{96,112},{112,128},... | collective-permute-start | bytes 49160 | tf_op jit(solution)/shard_map/ppermute | solution.py:87
  87.8 0.8 collective-permute-done.1.earlier_ref
  88.6 4.8 %shard_map.57 = bf16[16,8,12288]{2,1,0:T(8,128)(2,1)S(1)} custom-call(s32[96,2]{1,0:T(8,128)S(1)} %broadcast_subtract_fusion.slots_ref, bf16[64,128]{1,0:T(8,128)(2,1)S(1)} %collective-permute-done.1.earlier_ref, bf16[128,128]{1,0:T(8,128)(2,1)S(1)} %shard_map.56.coupled_ref, bf16[96,2,64,128]{3,2,1,0:T(8,128)(2,1)} %bitcast.18), custom_call_target="tpu_custom_call" | custom-call | flops 402653184 | bytes 6291456 | tf_op jit(solution)/shard_map/pallas_call | solution.py:141
  93.4 41.0 %all_to_all.25 = bf16[16,8,12288]{2,1,0:T(8,128)(2,1)S(1)} all-to-all(bf16[16,8,12288]{2,1,0:T(8,128)(2,1)S(1)} %shard_map.57), channel_id=1, replica_groups=mesh['band'=16,'grid'=16] {'grid'}, dimensions={0} | all-to-all | bytes 6291456 | tf_op jit(solution)/shard_map/all_to_all | solution.py:150
  134.4 1.7 %copy.8 = bf16[8,196608]{1,0:T(8,128)(2,1)} copy(bf16[8,196608]{1,0:T(8,128)(2,1)S(1)} %bitcast.19) | data formatting | bytes 6291456
  (8 shorter events, 0.0 us)
Async XLA Ops:
  0.0 6.9 %copy-start.1 = (s32[96,2]{0,1:T(2,128)S(1)}, s32[96,2]{0,1:T(2,128)}, u32[]{:S(2)}) copy-start(s32[96,2]{0,1:T(2,128)} %param.7) | copy-start | bytes 2308
  0.0 7.0 %copy-start = (f32[2,16,16]{2,1,0:T(8,128)S(1)}, f32[2,16,16]{2,1,0:T(8,128)}, u32[]{:S(2)}) copy-start(f32[2,16,16]{2,1,0:T(8,128)} %param.8) | copy-start | bytes 6148
  0.0 53.5 %all-to-all-start = ((bf16[8,16,12288]{2,0,1:T(8,128)(2,1)}), bf16[8,16,12288]{2,0,1:T(8,128)(2,1)S(1)}, u32[]{:S(2)}, u32[]{:S(2)}) async-start(bf16[8,16,12288]{2,0,1:T(8,128)(2,1)} %bitcast.20), calls=%async_computation | async-start | bytes 6291456 | tf_op jit(solution)/shard_map/all_to_all | solution.py:113
  53.5 9.5 %copy-start.2 = (s32[8]{0:T(128)S(1)}, s32[8]{0:T(128)}, u32[]{:S(2)}) copy-start(s32[8]{0:T(128)} %param.9) | copy-start | bytes 100
  59.3 7.9 %collective-permute-start = (bf16[64,128]{1,0:T(8,128)(2,1)S(1)}, bf16[64,128]{1,0:T(8,128)(2,1)S(1)}, u32[]{:S(2)}, u32[]{:S(2)}) collective-permute-start(bf16[64,128]{1,0:T(8,128)(2,1)S(1)} %get-tuple-element.8), channel_id=1, source_target_pairs={{16,0},{32,16},{48,32},{64,48},{80,64},{96,80},{112,96},{128,112},... | collective-permute-start | bytes 49160 | tf_op jit(solution)/shard_map/ppermute | solution.py:87
  68.1 13.9 %all-to-all-start.1 = ((bf16[16,128,128]{2,1,0:T(8,128)(2,1)}), bf16[16,128,128]{2,1,0:T(8,128)(2,1)S(1)}, u32[]{:S(2)}, u32[]{:S(2)}) async-start(bf16[16,128,128]{2,1,0:T(8,128)(2,1)} %broadcast_in_dim.55), calls=%async_computation.1 | async-start | bytes 1048576 | tf_op jit(solution)/shard_map/all_to_all | solution.py:131
  82.3 6.3 %collective-permute-start.1 = (bf16[64,128]{1,0:T(8,128)(2,1)S(1)}, bf16[64,128]{1,0:T(8,128)(2,1)S(1)}, u32[]{:S(2)}, u32[]{:S(2)}) collective-permute-start(bf16[64,128]{1,0:T(8,128)(2,1)S(1)} %slice.22), channel_id=1, source_target_pairs={{0,16},{16,32},{32,48},{48,64},{64,80},{80,96},{96,112},{112,128},... | collective-permute-start | bytes 49160 | tf_op jit(solution)/shard_map/ppermute | solution.py:87

commit v2 on v1

--- a/solution.py
+++ b/solution.py
@@ -8,7 +8,7 @@
 BLK = 2
 EDGE = 1
 SLOTS = BLK + EDGE
-VMEM_LIMIT = 48 * 1024 * 1024
+VMEM_LIMIT = 24 * 1024 * 1024
 
 
 def whole(space=pltpu.VMEM):
@@ -28,7 +28,11 @@
     )
 
 
-def forward_kernel(slots_ref, columns_ref, tiles_ref, own_ref, edge_ref, total):
+def slot_of(names_ref, r, j):
+    return names_ref[j, r] - (lax.axis_index("band") * BLK - EDGE)
+
+
+def forward_kernel(names_ref, columns_ref, tiles_ref, own_ref, edge_ref, total):
     rows, per_row, proj, tile = tiles_ref.shape
     groups, local, _ = columns_ref.shape
     bands = groups * local
@@ -42,7 +46,7 @@
             values, columns, (((1,), (1,)), ((), ())), preferred_element_type=jnp.float32
         )
         for j in range(per_row):
-            total[slots_ref[r, j]] += part[j * proj : (j + 1) * proj]
+            total[slot_of(names_ref, r, j)] += part[j * proj : (j + 1) * proj]
         return carry
 
     lax.fori_loop(0, rows, row, 0, unroll=8)
@@ -50,17 +54,31 @@
     edge_ref[...] = total[0].astype(edge_ref.dtype)
 
 
-def couple_kernel(parts_ref, mix_ref, coupled_ref):
-    count = parts_ref.shape[0]
-    summed = parts_ref[0].astype(jnp.float32)
-    for source in range(1, count):
-        summed = summed + parts_ref[source].astype(jnp.float32)
-    coupled_ref[...] = jnp.dot(
-        mix_ref[...], summed, precision=lax.Precision.HIGHEST, preferred_element_type=jnp.float32
-    ).astype(coupled_ref.dtype)
+def share_kernel(own_ref, later_ref, shared_ref):
+    last = own_ref.shape[0] - later_ref.shape[0]
+    kept = own_ref[:last].astype(shared_ref.dtype)
+    summed = (own_ref[last:] + later_ref[...].astype(jnp.float32)).astype(shared_ref.dtype)
+    for target in range(shared_ref.shape[0]):
+        shared_ref[target, :last] = kept
+        shared_ref[target, last:] = summed
 
 
-def backward_kernel(slots_ref, earlier_ref, coupled_ref, tiles_ref, out_ref, pairs):
+def couple_kernel(kinds_ref, parts_ref, couplings_ref, coupled_ref):
+    width = couplings_ref.shape[1]
+    summed = parts_ref[0].astype(jnp.float32)
+    for source in range(1, parts_ref.shape[0]):
+        summed = summed + parts_ref[source].astype(jnp.float32)
+    for atom in range(kinds_ref.shape[0]):
+        at = slice(atom * width, (atom + 1) * width)
+        coupled_ref[at] = jnp.dot(
+            couplings_ref[kinds_ref[atom]],
+            summed[at],
+            precision=lax.Precision.HIGHEST,
+            preferred_element_type=jnp.float32,
+        ).astype(coupled_ref.dtype)
+
+
+def backward_kernel(names_ref, earlier_ref, coupled_ref, tiles_ref, out_ref, pairs):
     rows, per_row, proj, tile = tiles_ref.shape
     groups, local, _ = out_ref.shape
     blocks = [earlier_ref[...]] + [coupled_ref[k * proj : (k + 1) * proj] for k in range(BLK)]
@@ -73,7 +91,7 @@
     def row(r, carry):
         at = pl.ds(pl.multiple_of(r * tile, tile), tile)
         values = tiles_ref[r].reshape(per_row * proj, tile)
-        chosen = pairs[slots_ref[r, 0] * SLOTS + slots_ref[r, 1]]
+        chosen = pairs[slot_of(names_ref, r, 0) * SLOTS + slot_of(names_ref, r, 1)]
         result = jnp.dot(chosen, values, preferred_element_type=jnp.float32)
         out_ref[:, :, at] = result.astype(out_ref.dtype).reshape(groups, local, tile)
         return carry
@@ -87,16 +105,6 @@
     return lax.ppermute(block, axis, route)
 
 
-def mixing(kinds, couplings):
-    atoms, width = kinds.shape[0], couplings.shape[1]
-    table = jnp.zeros((atoms, width, width), jnp.float32)
-    for kind in range(couplings.shape[0]):
-        table = table + jnp.where((kinds == kind)[:, None, None], couplings[kind], jnp.float32(0.0))
-    same = jnp.eye(atoms, dtype=jnp.bool_)[:, None, :, None]
-    spread = jnp.where(same, table[:, :, None, :], jnp.float32(0.0))
-    return spread.reshape(atoms * width, atoms * width)
-
-
 def body(psi, tiles, tile_block, couplings, species):
     splits = lax.axis_size("grid")
     local_bands, slab_points = psi.shape
@@ -105,9 +113,8 @@
     points = rows * tile
     flops = 2 * rows * per_row * proj * tile * bands
     moved = 2 * (bands * points + tiles.size)
-    slab = lax.axis_index("band")
-    slots = tile_block - (slab * BLK - EDGE)
-    mix = mixing(species, couplings)
+    last = (BLK - EDGE) * proj
+    names = tile_block.T
     values = jnp.transpose(tiles, (0, 1, 3, 2))
 
     spread = lax.all_to_all(
@@ -124,19 +131,21 @@
         [pltpu.VMEM((SLOTS, proj, bands), jnp.float32)],
         flops,
         moved,
-    )(slots, spread, values)
-    later = from_behind(edge, "band", -1).astype(jnp.float32)
-    last = (BLK - EDGE) * proj
-    own = jnp.concatenate([own[:last], own[last:] + later], axis=0).astype(jnp.bfloat16)
-    parts = lax.all_to_all(
-        jnp.broadcast_to(own[None], (splits,) + own.shape), "grid", 0, 0, tiled=True
-    )
+    )(names, spread, values)
+    later = from_behind(edge, "band", -1)
+    shared = call(
+        share_kernel,
+        jax.ShapeDtypeStruct((splits,) + own.shape, jnp.bfloat16),
+        (pltpu.VMEM, pltpu.VMEM),
+        pltpu.VMEM,
+    )(own, later)
+    parts = lax.all_to_all(shared, "grid", split_axis=0, concat_axis=0, tiled=True)
     coupled = call(
         couple_kernel,
         jax.ShapeDtypeStruct((BLK * proj, bands), jnp.bfloat16),
-        (pltpu.VMEM, pltpu.VMEM),
+        (pltpu.SMEM, pltpu.VMEM, pltpu.VMEM),
         pltpu.VMEM,
-    )(parts, mix)
+    )(species, parts, couplings)
     earlier = from_behind(coupled[last:], "band", 1)
     result = call(
         backward_kernel,
@@ -146,7 +155,7 @@
         [pltpu.VMEM((SLOTS * SLOTS, bands, per_row * proj), jnp.bfloat16)],
         flops,
         moved,
-    )(slots, earlier, coupled, values)
+    )(names, earlier, coupled, values)
     returned = lax.all_to_all(result, "grid", split_axis=0, concat_axis=0, tiled=True)
     return jnp.transpose(returned, (1, 0, 2)).reshape(local_bands, slab_points)
 

time: 137 us -> 124 us (0.905)
  blocking collectives: 41 us -> 99.2 us
  waiting for transfers between devices: 60.8 us -> 4.99 us
  starting transfers between devices: 20.2 us -> 9.33 us
  Pallas kernels: 10.8 us -> 8.68 us
    all_to_all x0 -> x2, blocking collectives: none -> 58.1 us  [the longest x1 45.6 us: body(): lax.all_to_all(psi.reshape(local_bands, splits, points), 'grid', split_ax...]
    all_to_all x2 -> x0, waiting for transfers between devices: 55.9 us -> none  [the longest x1 46.5 us: body(): lax.all_to_all(psi.reshape(local_bands, splits, points), 'grid', split_ax...]
    all_to_all x2 -> x0, starting transfers between devices: 11 us -> none  [the longest x1 6.89 us: body(): lax.all_to_all(psi.reshape(local_bands, splits, points), 'grid', split_ax...]
    pallas_call x1, Pallas kernels: 5.79 us -> 4.41 us  [body(): call(forward_kernel, (jax.ShapeDtypeStruct((BLK * proj, bands), jnp.float...]
  transfers between devices with their start and end apart: 4 -> 2, of which waited for: 4 -> 2; matrix products, arithmetic and copies ran while one was open for 0% -> 0% of each run, Pallas kernels for 0% -> 0%
where the time goes in v2:
time: 124 us
  blocking collectives  99.2 us (80%)
  starting transfers between devices  9.33 us (8%)
  Pallas kernels  8.68 us (7%)
  waiting for transfers between devices  4.99 us (4%)
  local copies, waits for them, and re-layouts  1.68 us (1%)
    all_to_all x1, blocking collectives, body(): lax.all_to_all(psi.reshape(local_bands, splits, points), 'grid', split_ax...  45.6 us
    all_to_all x1, blocking collectives, body(): lax.all_to_all(result, 'grid', split_axis=0, concat_axis=0, tiled=True)  41.1 us
    all_to_all x1, blocking collectives, body(): lax.all_to_all(shared, 'grid', split_axis=0, concat_axis=0, tiled=True)  12.5 us
    ppermute x2, starting transfers between devices, from_behind(): return lax.ppermute(block, axis, route)  9.33 us
    ppermute x2, waiting for transfers between devices, from_behind(): return lax.ppermute(block, axis, route)  4.99 us
    pallas_call x1, Pallas kernels, body(): call(forward_kernel, (jax.ShapeDtypeStruct((BLK * proj, bands), jnp.float...  4.41 us
    pallas_call x1, Pallas kernels, body(): call(backward_kernel, jax.ShapeDtypeStruct((splits, local_bands, points),...  3.44 us
  transfers between devices with their start and end apart: 2, of which 2 were waited for; matrix products, arithmetic and copies ran while one was open for 0% of the time, Pallas kernels for 0%

profile of v2, /device:TPU:97, one launch (start us, length us, event | category | flops | bytes accessed | tf_op | source)
XLA Modules:
  0.0 123.9 jit_solution(18184737076536792805)
XLA Ops:
  0.0 0.0 copy-start
  0.0 0.0 copy-start.2
  0.0 45.6 %all_to_all.25 = bf16[8,16,12288]{2,0,1:T(8,128)(2,1)S(1)} all-to-all(bf16[8,16,12288]{2,0,1:T(8,128)(2,1)} %bitcast.17), channel_id=1, replica_groups=mesh['band'=16,'grid'=16] {'grid'}, dimensions={1} | all-to-all | bytes 6291456 | tf_op jit(solution)/shard_map/all_to_all | solution.py:120
  45.6 0.0 copy-done
  45.6 0.0 copy-done.2
  45.6 0.0 copy-start.1
  45.6 0.0 copy-start.3
  45.6 4.4 %shard_map.55 = (f32[128,128]{1,0:T(8,128)S(1)}, bf16[64,128]{1,0:T(8,128)(2,1)S(1)}) custom-call(s32[2,96]{1,0:T(2,128)S(1)} %bitcast.14, bf16[16,8,12288]{2,1,0:T(8,128)(2,1)S(1)} %bitcast.11, bf16[96,2,64,128]{3,2,1,0:T(8,128)(2,1)S(1)} %bitcast.12), custom_call_target="tpu_custom_call" | custom-call | flops 402653184 | bytes 6291456 | tf_op jit(solution)/shard_map/pallas_call | solution.py:123
  50.1 3.9 %collective-permute-start = (bf16[64,128]{1,0:T(8,128)(2,1)S(1)}, bf16[64,128]{1,0:T(8,128)(2,1)S(1)}, u32[]{:S(2)}, u32[]{:S(2)}) collective-permute-start(bf16[64,128]{1,0:T(8,128)(2,1)S(1)} %get-tuple-element.8), channel_id=1, source_target_pairs={{16,0},{32,16},{48,32},{64,48},{80,64},{96,80},{112,96},{128,112},... | collective-permute-start | bytes 49160 | tf_op jit(solution)/shard_map/ppermute | solution.py:105
  53.9 4.1 %collective-permute-done.later_ref = bf16[64,128]{1,0:T(8,128)(2,1)S(1)} collective-permute-done((bf16[64,128]{1,0:T(8,128)(2,1)S(1)}, bf16[64,128]{1,0:T(8,128)(2,1)S(1)}, u32[]{:S(2)}, u32[]{:S(2)}) %collective-permute-start) | collective-permute-done | bytes 16416 | tf_op jit(solution)/shard_map/ppermute | solution.py:105
  58.1 12.5 %all_to_all.26.parts_ref = bf16[16,128,128]{2,1,0:T(8,128)(2,1)S(1)} all-to-all(bf16[16,128,128]{2,1,0:T(8,128)(2,1)S(1)} %shard_map.56), channel_id=1, replica_groups=mesh['band'=16,'grid'=16] {'grid'}, dimensions={0} | all-to-all | bytes 1048576 | tf_op jit(solution)/shard_map/all_to_all | solution.py:142
  70.6 0.0 copy-done.1
  70.6 0.0 copy-done.3
  70.6 0.8 shard_map.57.coupled_ref
  71.4 5.4 %collective-permute-start.1 = (bf16[64,128]{1,0:T(8,128)(2,1)S(1)}, bf16[64,128]{1,0:T(8,128)(2,1)S(1)}, u32[]{:S(2)}, u32[]{:S(2)}) collective-permute-start(bf16[64,128]{1,0:T(8,128)(2,1)S(1)} %slice.4), channel_id=1, source_target_pairs={{0,16},{16,32},{32,48},{48,64},{64,80},{80,96},{96,112},{112,128},... | collective-permute-start | bytes 49160 | tf_op jit(solution)/shard_map/ppermute | solution.py:105
  76.9 0.8 collective-permute-done.1.earlier_ref
  77.7 3.4 %shard_map.58 = bf16[16,8,12288]{2,1,0:T(8,128)(2,1)S(1)} custom-call(s32[2,96]{1,0:T(2,128)S(1)} %bitcast.15, bf16[64,128]{1,0:T(8,128)(2,1)S(1)} %collective-permute-done.1.earlier_ref, bf16[128,128]{1,0:T(8,128)(2,1)S(1)} %shard_map.57.coupled_ref, bf16[96,2,64,128]{3,2,1,0:T(8,128)(2,1)S(1)} %bitcast.13), custom_call_target="tpu_custom_call" | custom-call | flops 402653184 | bytes 6291456 | tf_op jit(solution)/shard_map/pallas_call | solution.py:150
  81.2 41.1 %all_to_all.27 = bf16[16,8,12288]{2,1,0:T(8,128)(2,1)S(1)} all-to-all(bf16[16,8,12288]{2,1,0:T(8,128)(2,1)S(1)} %shard_map.58), channel_id=1, replica_groups=mesh['band'=16,'grid'=16] {'grid'}, dimensions={0} | all-to-all | bytes 6291456 | tf_op jit(solution)/shard_map/all_to_all | solution.py:159
  122.3 1.7 %copy.7 = bf16[8,196608]{1,0:T(8,128)(2,1)} copy(bf16[8,196608]{1,0:T(8,128)(2,1)S(1)} %bitcast.16) | data formatting | bytes 6291456
  (2 shorter events, 0.0 us)
Async XLA Ops:
  0.0 45.6 %copy-start = (bf16[96,2,128,64]{2,3,1,0:T(8,128)(2,1)S(1)}, bf16[96,2,128,64]{2,3,1,0:T(8,128)(2,1)}, u32[]{:S(2)}) copy-start(bf16[96,2,128,64]{2,3,1,0:T(8,128)(2,1)} %param.6) | copy-start | bytes 9437188
  0.0 45.6 %copy-start.2 = (s32[96,2]{0,1:T(2,128)S(1)}, s32[96,2]{0,1:T(2,128)}, u32[]{:S(2)}) copy-start(s32[96,2]{0,1:T(2,128)} %param.7) | copy-start | bytes 2308
  45.6 25.0 %copy-start.1 = (f32[2,16,16]{2,1,0:T(8,128)S(1)}, f32[2,16,16]{2,1,0:T(8,128)}, u32[]{:S(2)}) copy-start(f32[2,16,16]{2,1,0:T(8,128)} %couplings_ref.1) | copy-start | bytes 6148
  45.6 25.0 %copy-start.3 = (s32[8]{0:T(128)S(1)}, s32[8]{0:T(128)}, u32[]{:S(2)}) copy-start(s32[8]{0:T(128)} %kinds_ref.1) | copy-start | bytes 100
  50.1 8.0 %collective-permute-start = (bf16[64,128]{1,0:T(8,128)(2,1)S(1)}, bf16[64,128]{1,0:T(8,128)(2,1)S(1)}, u32[]{:S(2)}, u32[]{:S(2)}) collective-permute-start(bf16[64,128]{1,0:T(8,128)(2,1)S(1)} %get-tuple-element.8), channel_id=1, source_target_pairs={{16,0},{32,16},{48,32},{64,48},{80,64},{96,80},{112,96},{128,112},... | collective-permute-start | bytes 49160 | tf_op jit(solution)/shard_map/ppermute | solution.py:105
  71.4 6.3 %collective-permute-start.1 = (bf16[64,128]{1,0:T(8,128)(2,1)S(1)}, bf16[64,128]{1,0:T(8,128)(2,1)S(1)}, u32[]{:S(2)}, u32[]{:S(2)}) collective-permute-start(bf16[64,128]{1,0:T(8,128)(2,1)S(1)} %slice.4), channel_id=1, source_target_pairs={{0,16},{16,32},{32,48},{48,64},{64,80},{80,96},{96,112},{112,128},... | collective-permute-start | bytes 49160 | tf_op jit(solution)/shard_map/ppermute | solution.py:105

commit v3 on v2

--- a/solution.py
+++ b/solution.py
@@ -34,22 +34,34 @@
 
 def forward_kernel(names_ref, columns_ref, tiles_ref, own_ref, edge_ref, total):
     rows, per_row, proj, tile = tiles_ref.shape
-    groups, local, _ = columns_ref.shape
-    bands = groups * local
+    points = rows * tile
+    groups = columns_ref.shape[1] // points
+    bands = groups * columns_ref.shape[0]
+    depth = per_row * proj
     total[...] = jnp.zeros_like(total)
 
-    def row(r, carry):
-        at = pl.ds(pl.multiple_of(r * tile, tile), tile)
-        columns = columns_ref[:, :, at].reshape(bands, tile)
-        values = tiles_ref[r].reshape(per_row * proj, tile)
+    def pair(step, carry):
+        columns = jnp.concatenate(
+            [
+                columns_ref[:, pl.ds(pl.multiple_of(g * points + (step * 2 + row) * tile, tile), tile)]
+                for row in range(2)
+                for g in range(groups)
+            ],
+            axis=0,
+        )
+        values = tiles_ref[pl.ds(step * 2, 2)].reshape(2 * depth, tile)
         part = lax.dot_general(
             values, columns, (((1,), (1,)), ((), ())), preferred_element_type=jnp.float32
         )
-        for j in range(per_row):
-            total[slot_of(names_ref, r, j)] += part[j * proj : (j + 1) * proj]
+        for row in range(2):
+            for j in range(per_row):
+                first = row * depth + j * proj
+                total[slot_of(names_ref, step * 2 + row, j)] += part[
+                    first : first + proj, row * bands : (row + 1) * bands
+                ]
         return carry
 
-    lax.fori_loop(0, rows, row, 0, unroll=8)
+    lax.fori_loop(0, rows // 2, pair, 0, unroll=rows // 2)
     own_ref[...] = total[EDGE:].reshape(own_ref.shape)
     edge_ref[...] = total[0].astype(edge_ref.dtype)
 
@@ -80,7 +92,9 @@
 
 def backward_kernel(names_ref, earlier_ref, coupled_ref, tiles_ref, out_ref, pairs):
     rows, per_row, proj, tile = tiles_ref.shape
-    groups, local, _ = out_ref.shape
+    points = rows * tile
+    groups = out_ref.shape[1] // points
+    local = out_ref.shape[0]
     blocks = [earlier_ref[...]] + [coupled_ref[k * proj : (k + 1) * proj] for k in range(BLK)]
     blocks = [b.astype(jnp.float32) for b in blocks]
     for first in range(SLOTS):
@@ -89,14 +103,16 @@
             pairs[first * SLOTS + second] = both.T.astype(pairs.dtype)
 
     def row(r, carry):
-        at = pl.ds(pl.multiple_of(r * tile, tile), tile)
         values = tiles_ref[r].reshape(per_row * proj, tile)
         chosen = pairs[slot_of(names_ref, r, 0) * SLOTS + slot_of(names_ref, r, 1)]
         result = jnp.dot(chosen, values, preferred_element_type=jnp.float32)
-        out_ref[:, :, at] = result.astype(out_ref.dtype).reshape(groups, local, tile)
+        result = result.astype(out_ref.dtype)
+        for g in range(groups):
+            at = pl.ds(pl.multiple_of(g * points + r * tile, tile), tile)
+            out_ref[:, at] = result[g * local : (g + 1) * local]
         return carry
 
-    lax.fori_loop(0, rows, row, 0, unroll=8)
+    lax.fori_loop(0, rows, row, 0, unroll=rows)
 
 
 def from_behind(block, axis, distance):
@@ -107,7 +123,7 @@
 
 def body(psi, tiles, tile_block, couplings, species):
     splits = lax.axis_size("grid")
-    local_bands, slab_points = psi.shape
+    local_bands = psi.shape[0]
     rows, per_row, tile, proj = tiles.shape
     bands = local_bands * splits
     points = rows * tile
@@ -117,9 +133,7 @@
     names = tile_block.T
     values = jnp.transpose(tiles, (0, 1, 3, 2))
 
-    spread = lax.all_to_all(
-        psi.reshape(local_bands, splits, points), "grid", split_axis=1, concat_axis=0, tiled=True
-    ).reshape(splits, local_bands, points)
+    spread = lax.all_to_all(psi, "grid", split_axis=1, concat_axis=1, tiled=True)
     own, edge = call(
         forward_kernel,
         (
@@ -149,15 +163,14 @@
     earlier = from_behind(coupled[last:], "band", 1)
     result = call(
         backward_kernel,
-        jax.ShapeDtypeStruct((splits, local_bands, points), jnp.bfloat16),
+        jax.ShapeDtypeStruct(psi.shape, jnp.bfloat16),
         (pltpu.SMEM, pltpu.VMEM, pltpu.VMEM, pltpu.VMEM),
         pltpu.VMEM,
         [pltpu.VMEM((SLOTS * SLOTS, bands, per_row * proj), jnp.bfloat16)],
         flops,
         moved,
     )(names, earlier, coupled, values)
-    returned = lax.all_to_all(result, "grid", split_axis=0, concat_axis=0, tiled=True)
-    return jnp.transpose(returned, (1, 0, 2)).reshape(local_bands, slab_points)
+    return lax.all_to_all(result, "grid", split_axis=1, concat_axis=1, tiled=True)
 
 
 def solution(mesh):

time: 124 us -> 121 us (0.976)
  Pallas kernels: 8.68 us -> 5.07 us
    pallas_call x1, Pallas kernels: 4.41 us -> 2.46 us  [body(): call(forward_kernel, (jax.ShapeDtypeStruct((BLK * proj, bands), jnp.float...]
    pallas_call x1, Pallas kernels: 3.44 us -> 1.78 us  [body(): call(backward_kernel, jax.ShapeDtypeStruct(psi.shape, jnp.bfloat16), (plt...]
where the time goes in v3:
time: 121 us; the launch traced here: 120 us
  blocking collectives  99.2 us (82%)
  starting transfers between devices  9.34 us (8%)
  Pallas kernels  5.07 us (4%)
  waiting for transfers between devices  5 us (4%)
  local copies, waits for them, and re-layouts  1.68 us (1%)
    all_to_all x1, blocking collectives, body(): lax.all_to_all(psi, 'grid', split_axis=1, concat_axis=1, tiled=True)  45.6 us
    all_to_all x1, blocking collectives, body(): lax.all_to_all(result, 'grid', split_axis=1, concat_axis=1, tiled=True)  41.1 us
    all_to_all x1, blocking collectives, body(): lax.all_to_all(shared, 'grid', split_axis=0, concat_axis=0, tiled=True)  12.5 us
    ppermute x2, starting transfers between devices, from_behind(): return lax.ppermute(block, axis, route)  9.34 us
    ppermute x2, waiting for transfers between devices, from_behind(): return lax.ppermute(block, axis, route)  5 us
    pallas_call x1, Pallas kernels, body(): call(forward_kernel, (jax.ShapeDtypeStruct((BLK * proj, bands), jnp.float...  2.46 us
  transfers between devices with their start and end apart: 2, of which 2 were waited for; matrix products, arithmetic and copies ran while one was open for 0% of the time, Pallas kernels for 0%

profile of v3, /device:TPU:97, one launch (start us, length us, event | category | flops | bytes accessed | tf_op | source)
XLA Modules:
  0.0 120.3 jit_solution(4206842995430570861)
XLA Ops:
  0.0 0.0 copy-start
  0.0 0.0 copy-start.2
  0.0 45.6 %all_to_all.28 = bf16[8,16,12288]{2,0,1:T(8,128)(2,1)S(1)} all-to-all(bf16[8,16,12288]{2,0,1:T(8,128)(2,1)} %bitcast.13), channel_id=1, replica_groups=mesh['band'=16,'grid'=16] {'grid'}, dimensions={1} | all-to-all | bytes 6291456 | tf_op jit(solution)/shard_map/all_to_all | solution.py:136
  45.6 0.0 copy-done
  45.6 0.0 copy-done.2
  45.6 0.0 copy-start.1
  45.6 0.0 copy-start.3
  45.6 2.5 %shard_map.55 = (f32[128,128]{1,0:T(8,128)S(1)}, bf16[64,128]{1,0:T(8,128)(2,1)S(1)}) custom-call(s32[2,96]{1,0:T(2,128)S(1)} %bitcast.10, bf16[8,196608]{1,0:T(8,128)(2,1)S(1)} %bitcast.6, bf16[96,2,64,128]{3,2,1,0:T(8,128)(2,1)S(1)} %bitcast.8), custom_call_target="tpu_custom_call" | custom-call | flops 402653184 | bytes 6291456 | tf_op jit(solution)/shard_map/pallas_call | solution.py:137
  48.1 3.9 %collective-permute-start = (bf16[64,128]{1,0:T(8,128)(2,1)S(1)}, bf16[64,128]{1,0:T(8,128)(2,1)S(1)}, u32[]{:S(2)}, u32[]{:S(2)}) collective-permute-start(bf16[64,128]{1,0:T(8,128)(2,1)S(1)} %get-tuple-element.8), channel_id=1, source_target_pairs={{16,0},{32,16},{48,32},{64,48},{80,64},{96,80},{112,96},{128,112},... | collective-permute-start | bytes 49160 | tf_op jit(solution)/shard_map/ppermute | solution.py:121
  52.0 4.1 %collective-permute-done.later_ref = bf16[64,128]{1,0:T(8,128)(2,1)S(1)} collective-permute-done((bf16[64,128]{1,0:T(8,128)(2,1)S(1)}, bf16[64,128]{1,0:T(8,128)(2,1)S(1)}, u32[]{:S(2)}, u32[]{:S(2)}) %collective-permute-start) | collective-permute-done | bytes 16416 | tf_op jit(solution)/shard_map/ppermute | solution.py:121
  56.2 12.5 %all_to_all.29.parts_ref = bf16[16,128,128]{2,1,0:T(8,128)(2,1)S(1)} all-to-all(bf16[16,128,128]{2,1,0:T(8,128)(2,1)S(1)} %shard_map.56), channel_id=1, replica_groups=mesh['band'=16,'grid'=16] {'grid'}, dimensions={0} | all-to-all | bytes 1048576 | tf_op jit(solution)/shard_map/all_to_all | solution.py:156
  68.7 0.0 copy-done.1
  68.7 0.0 copy-done.3
  68.7 0.8 shard_map.57.coupled_ref
  69.5 5.5 %collective-permute-start.1 = (bf16[64,128]{1,0:T(8,128)(2,1)S(1)}, bf16[64,128]{1,0:T(8,128)(2,1)S(1)}, u32[]{:S(2)}, u32[]{:S(2)}) collective-permute-start(bf16[64,128]{1,0:T(8,128)(2,1)S(1)} %slice.4), channel_id=1, source_target_pairs={{0,16},{16,32},{32,48},{48,64},{64,80},{80,96},{96,112},{112,128},... | collective-permute-start | bytes 49160 | tf_op jit(solution)/shard_map/ppermute | solution.py:121
  75.0 0.8 collective-permute-done.1.earlier_ref
  75.8 1.8 %shard_map.58 = bf16[8,196608]{1,0:T(8,128)(2,1)S(1)} custom-call(s32[2,96]{1,0:T(2,128)S(1)} %bitcast.11, bf16[64,128]{1,0:T(8,128)(2,1)S(1)} %collective-permute-done.1.earlier_ref, bf16[128,128]{1,0:T(8,128)(2,1)S(1)} %shard_map.57.coupled_ref, bf16[96,2,64,128]{3,2,1,0:T(8,128)(2,1)S(1)} %bitcast.9), custom_call_target="tpu_custom_call" | custom-call | flops 402653184 | bytes 6291456 | tf_op jit(solution)/shard_map/pallas_call | solution.py:164
  77.6 41.1 %all_to_all.30 = bf16[8,16,12288]{2,0,1:T(8,128)(2,1)S(1)} all-to-all(bf16[8,16,12288]{2,0,1:T(8,128)(2,1)S(1)} %bitcast.7), channel_id=1, replica_groups=mesh['band'=16,'grid'=16] {'grid'}, dimensions={1} | all-to-all | bytes 6291456 | tf_op jit(solution)/shard_map/all_to_all | solution.py:173
  118.7 1.7 %copy.7 = bf16[8,196608]{1,0:T(8,128)(2,1)} copy(bf16[8,196608]{1,0:T(8,128)(2,1)S(1)} %bitcast.12) | data formatting | bytes 6291456
  (2 shorter events, 0.0 us)
Async XLA Ops:
  0.0 45.6 %copy-start = (bf16[96,2,128,64]{2,3,1,0:T(8,128)(2,1)S(1)}, bf16[96,2,128,64]{2,3,1,0:T(8,128)(2,1)}, u32[]{:S(2)}) copy-start(bf16[96,2,128,64]{2,3,1,0:T(8,128)(2,1)} %param.6) | copy-start | bytes 9437188
  0.0 45.6 %copy-start.2 = (s32[96,2]{0,1:T(2,128)S(1)}, s32[96,2]{0,1:T(2,128)}, u32[]{:S(2)}) copy-start(s32[96,2]{0,1:T(2,128)} %param.7) | copy-start | bytes 2308
  45.6 23.1 %copy-start.1 = (f32[2,16,16]{2,1,0:T(8,128)S(1)}, f32[2,16,16]{2,1,0:T(8,128)}, u32[]{:S(2)}) copy-start(f32[2,16,16]{2,1,0:T(8,128)} %couplings_ref.1) | copy-start | bytes 6148
  45.6 23.1 %copy-start.3 = (s32[8]{0:T(128)S(1)}, s32[8]{0:T(128)}, u32[]{:S(2)}) copy-start(s32[8]{0:T(128)} %kinds_ref.1) | copy-start | bytes 100
  48.1 8.0 %collective-permute-start = (bf16[64,128]{1,0:T(8,128)(2,1)S(1)}, bf16[64,128]{1,0:T(8,128)(2,1)S(1)}, u32[]{:S(2)}, u32[]{:S(2)}) collective-permute-start(bf16[64,128]{1,0:T(8,128)(2,1)S(1)} %get-tuple-element.8), channel_id=1, source_target_pairs={{16,0},{32,16},{48,32},{64,48},{80,64},{96,80},{112,96},{128,112},... | collective-permute-start | bytes 49160 | tf_op jit(solution)/shard_map/ppermute | solution.py:121
  69.5 6.3 %collective-permute-start.1 = (bf16[64,128]{1,0:T(8,128)(2,1)S(1)}, bf16[64,128]{1,0:T(8,128)(2,1)S(1)}, u32[]{:S(2)}, u32[]{:S(2)}) collective-permute-start(bf16[64,128]{1,0:T(8,128)(2,1)S(1)} %slice.4), channel_id=1, source_target_pairs={{0,16},{16,32},{32,48},{48,64},{64,80},{80,96},{96,112},{112,128},... | collective-permute-start | bytes 49160 | tf_op jit(solution)/shard_map/ppermute | solution.py:121

commit v4 on v3

--- a/solution.py
+++ b/solution.py
@@ -116,9 +116,8 @@
 
 
 def from_behind(block, axis, distance):
-    devices = range(lax.axis_size(axis))
-    route = [(i - distance, i) for i in devices if i - distance in devices]
-    return lax.ppermute(block, axis, route)
+    size = lax.axis_size(axis)
+    return lax.ppermute(block, axis, [(i, (i + distance) % size) for i in range(size)])
 
 
 def body(psi, tiles, tile_block, couplings, species):

time: 121 us -> 117 us (0.967)
  starting transfers between devices: 9.34 us -> 5.56 us
    ppermute x2, starting transfers between devices: 9.34 us -> 5.56 us  [from_behind(): lax.ppermute(block, axis, [(i, (i + distance) % size) for i in range(size)])]
where the time goes in v4:
time: 117 us
  blocking collectives  99.1 us (85%)
  starting transfers between devices  5.56 us (5%)
  Pallas kernels  5.08 us (4%)
  waiting for transfers between devices  5.03 us (4%)
  local copies, waits for them, and re-layouts  1.68 us (1%)
    all_to_all x1, blocking collectives, body(): lax.all_to_all(psi, 'grid', split_axis=1, concat_axis=1, tiled=True)  45.6 us
    all_to_all x1, blocking collectives, body(): lax.all_to_all(result, 'grid', split_axis=1, concat_axis=1, tiled=True)  41 us
    all_to_all x1, blocking collectives, body(): lax.all_to_all(shared, 'grid', split_axis=0, concat_axis=0, tiled=True)  12.5 us
    ppermute x2, starting transfers between devices, from_behind(): lax.ppermute(block, axis, [(i, (i + distance) % size) for i in range(size)])  5.56 us
    ppermute x2, waiting for transfers between devices, from_behind(): lax.ppermute(block, axis, [(i, (i + distance) % size) for i in range(size)])  5.03 us
    pallas_call x1, Pallas kernels, body(): call(forward_kernel, (jax.ShapeDtypeStruct((BLK * proj, bands), jnp.float...  2.47 us
  transfers between devices with their start and end apart: 2, of which 2 were waited for; matrix products, arithmetic and copies ran while one was open for 0% of the time, Pallas kernels for 0%

profile of v4, /device:TPU:97, one launch (start us, length us, event | category | flops | bytes accessed | tf_op | source)
XLA Modules:
  0.0 116.5 jit_solution(1949898151500014964)
XLA Ops:
  0.0 0.0 copy-start
  0.0 0.0 copy-start.2
  0.0 45.6 %all_to_all.28 = bf16[8,16,12288]{2,0,1:T(8,128)(2,1)S(1)} all-to-all(bf16[8,16,12288]{2,0,1:T(8,128)(2,1)} %bitcast.13), channel_id=1, replica_groups=mesh['band'=16,'grid'=16] {'grid'}, dimensions={1} | all-to-all | bytes 6291456 | tf_op jit(solution)/shard_map/all_to_all | solution.py:135
  45.6 0.0 copy-done
  45.6 0.0 copy-done.2
  45.6 0.0 copy-start.1
  45.6 0.0 copy-start.3
  45.6 2.5 %shard_map.55 = (f32[128,128]{1,0:T(8,128)S(1)}, bf16[64,128]{1,0:T(8,128)(2,1)S(1)}) custom-call(s32[2,96]{1,0:T(2,128)S(1)} %bitcast.10, bf16[8,196608]{1,0:T(8,128)(2,1)S(1)} %bitcast.6, bf16[96,2,64,128]{3,2,1,0:T(8,128)(2,1)S(1)} %bitcast.8), custom_call_target="tpu_custom_call" | custom-call | flops 402653184 | bytes 6291456 | tf_op jit(solution)/shard_map/pallas_call | solution.py:136
  48.1 2.0 %collective-permute-start = (bf16[64,128]{1,0:T(8,128)(2,1)S(1)}, bf16[64,128]{1,0:T(8,128)(2,1)S(1)}, u32[]{:S(2)}, u32[]{:S(2)}) collective-permute-start(bf16[64,128]{1,0:T(8,128)(2,1)S(1)} %get-tuple-element.8), channel_id=1, source_target_pairs={{0,240},{16,0},{32,16},{48,32},{64,48},{80,64},{96,80},{112,96},{1... | collective-permute-start | bytes 49160 | tf_op jit(solution)/shard_map/ppermute | solution.py:120
  50.1 4.2 %collective-permute-done.later_ref = bf16[64,128]{1,0:T(8,128)(2,1)S(1)} collective-permute-done((bf16[64,128]{1,0:T(8,128)(2,1)S(1)}, bf16[64,128]{1,0:T(8,128)(2,1)S(1)}, u32[]{:S(2)}, u32[]{:S(2)}) %collective-permute-start) | collective-permute-done | bytes 16416 | tf_op jit(solution)/shard_map/ppermute | solution.py:120
  54.3 12.5 %all_to_all.29.parts_ref = bf16[16,128,128]{2,1,0:T(8,128)(2,1)S(1)} all-to-all(bf16[16,128,128]{2,1,0:T(8,128)(2,1)S(1)} %shard_map.56), channel_id=1, replica_groups=mesh['band'=16,'grid'=16] {'grid'}, dimensions={0} | all-to-all | bytes 1048576 | tf_op jit(solution)/shard_map/all_to_all | solution.py:155
  66.8 0.0 copy-done.1
  66.8 0.0 copy-done.3
  66.8 0.8 shard_map.57.coupled_ref
  67.6 3.6 %collective-permute-start.1 = (bf16[64,128]{1,0:T(8,128)(2,1)S(1)}, bf16[64,128]{1,0:T(8,128)(2,1)S(1)}, u32[]{:S(2)}, u32[]{:S(2)}) collective-permute-start(bf16[64,128]{1,0:T(8,128)(2,1)S(1)} %slice.4), channel_id=1, source_target_pairs={{0,16},{16,32},{32,48},{48,64},{64,80},{80,96},{96,112},{112,128},... | collective-permute-start | bytes 49160 | tf_op jit(solution)/shard_map/ppermute | solution.py:120
  71.2 0.9 collective-permute-done.1.earlier_ref
  72.0 1.8 %shard_map.58 = bf16[8,196608]{1,0:T(8,128)(2,1)S(1)} custom-call(s32[2,96]{1,0:T(2,128)S(1)} %bitcast.11, bf16[64,128]{1,0:T(8,128)(2,1)S(1)} %collective-permute-done.1.earlier_ref, bf16[128,128]{1,0:T(8,128)(2,1)S(1)} %shard_map.57.coupled_ref, bf16[96,2,64,128]{3,2,1,0:T(8,128)(2,1)S(1)} %bitcast.9), custom_call_target="tpu_custom_call" | custom-call | flops 402653184 | bytes 6291456 | tf_op jit(solution)/shard_map/pallas_call | solution.py:163
  73.8 41.0 %all_to_all.30 = bf16[8,16,12288]{2,0,1:T(8,128)(2,1)S(1)} all-to-all(bf16[8,16,12288]{2,0,1:T(8,128)(2,1)S(1)} %bitcast.7), channel_id=1, replica_groups=mesh['band'=16,'grid'=16] {'grid'}, dimensions={1} | all-to-all | bytes 6291456 | tf_op jit(solution)/shard_map/all_to_all | solution.py:172
  114.9 1.7 %copy.7 = bf16[8,196608]{1,0:T(8,128)(2,1)} copy(bf16[8,196608]{1,0:T(8,128)(2,1)S(1)} %bitcast.12) | data formatting | bytes 6291456
  (2 shorter events, 0.0 us)
Async XLA Ops:
  0.0 45.6 %copy-start = (bf16[96,2,128,64]{2,3,1,0:T(8,128)(2,1)S(1)}, bf16[96,2,128,64]{2,3,1,0:T(8,128)(2,1)}, u32[]{:S(2)}) copy-start(bf16[96,2,128,64]{2,3,1,0:T(8,128)(2,1)} %param.6) | copy-start | bytes 9437188
  0.0 45.6 %copy-start.2 = (s32[96,2]{0,1:T(2,128)S(1)}, s32[96,2]{0,1:T(2,128)}, u32[]{:S(2)}) copy-start(s32[96,2]{0,1:T(2,128)} %param.7) | copy-start | bytes 2308
  45.6 21.2 %copy-start.1 = (f32[2,16,16]{2,1,0:T(8,128)S(1)}, f32[2,16,16]{2,1,0:T(8,128)}, u32[]{:S(2)}) copy-start(f32[2,16,16]{2,1,0:T(8,128)} %couplings_ref.1) | copy-start | bytes 6148
  45.6 21.2 %copy-start.3 = (s32[8]{0:T(128)S(1)}, s32[8]{0:T(128)}, u32[]{:S(2)}) copy-start(s32[8]{0:T(128)} %kinds_ref.1) | copy-start | bytes 100
  48.1 6.1 %collective-permute-start = (bf16[64,128]{1,0:T(8,128)(2,1)S(1)}, bf16[64,128]{1,0:T(8,128)(2,1)S(1)}, u32[]{:S(2)}, u32[]{:S(2)}) collective-permute-start(bf16[64,128]{1,0:T(8,128)(2,1)S(1)} %get-tuple-element.8), channel_id=1, source_target_pairs={{0,240},{16,0},{32,16},{48,32},{64,48},{80,64},{96,80},{112,96},{1... | collective-permute-start | bytes 49160 | tf_op jit(solution)/shard_map/ppermute | solution.py:120
  67.6 4.4 %collective-permute-start.1 = (bf16[64,128]{1,0:T(8,128)(2,1)S(1)}, bf16[64,128]{1,0:T(8,128)(2,1)S(1)}, u32[]{:S(2)}, u32[]{:S(2)}) collective-permute-start(bf16[64,128]{1,0:T(8,128)(2,1)S(1)} %slice.4), channel_id=1, source_target_pairs={{0,16},{16,32},{32,48},{48,64},{64,80},{80,96},{96,112},{112,128},... | collective-permute-start | bytes 49160 | tf_op jit(solution)/shard_map/ppermute | solution.py:120

commit v5 on v4

--- a/solution.py
+++ b/solution.py
@@ -8,6 +8,7 @@
 BLK = 2
 EDGE = 1
 SLOTS = BLK + EDGE
+AHEAD = 8
 VMEM_LIMIT = 24 * 1024 * 1024
 
 
@@ -32,7 +33,27 @@
     return names_ref[j, r] - (lax.axis_index("band") * BLK - EDGE)
 
 
-def forward_kernel(names_ref, columns_ref, tiles_ref, own_ref, edge_ref, total):
+def forward_kernel(
+    names_any,
+    kinds_any,
+    columns_ref,
+    tiles_ref,
+    couplings_ref,
+    own_ref,
+    edge_ref,
+    matrices_ref,
+    total,
+    early,
+    names_ref,
+    kinds_ref,
+    sems,
+):
+    copies = [
+        pltpu.make_async_copy(names_any, names_ref, sems.at[0]),
+        pltpu.make_async_copy(kinds_any, kinds_ref, sems.at[1]),
+    ]
+    for copy in copies:
+        copy.start()
     rows, per_row, proj, tile = tiles_ref.shape
     points = rows * tile
     groups = columns_ref.shape[1] // points
@@ -40,7 +61,7 @@
     depth = per_row * proj
     total[...] = jnp.zeros_like(total)
 
-    def pair(step, carry):
+    def products(step):
         columns = jnp.concatenate(
             [
                 columns_ref[:, pl.ds(pl.multiple_of(g * points + (step * 2 + row) * tile, tile), tile)]
@@ -53,17 +74,30 @@
         part = lax.dot_general(
             values, columns, (((1,), (1,)), ((), ())), preferred_element_type=jnp.float32
         )
-        for row in range(2):
-            for j in range(per_row):
-                first = row * depth + j * proj
-                total[slot_of(names_ref, step * 2 + row, j)] += part[
-                    first : first + proj, row * bands : (row + 1) * bands
-                ]
+        return part[:depth, :bands], part[depth:, bands:]
+
+    def add(r, part):
+        for j in range(per_row):
+            total[slot_of(names_ref, r, j)] += part[j * proj : (j + 1) * proj]
+
+    def pair(step, carry):
+        for row, part in enumerate(products(step)):
+            add(step * 2 + row, part)
         return carry
 
-    lax.fori_loop(0, rows // 2, pair, 0, unroll=rows // 2)
+    ahead = early.shape[0] // 2
+    for step in range(ahead):
+        for row, part in enumerate(products(step)):
+            early[step * 2 + row] = part
+    for copy in copies:
+        copy.wait()
+    for r in range(2 * ahead):
+        add(r, early[r])
+    lax.fori_loop(ahead, rows // 2, pair, 0, unroll=rows // 2 - ahead)
     own_ref[...] = total[EDGE:].reshape(own_ref.shape)
     edge_ref[...] = total[0].astype(edge_ref.dtype)
+    for atom in range(kinds_ref.shape[0]):
+        matrices_ref[atom] = couplings_ref[kinds_ref[atom]]
 
 
 def share_kernel(own_ref, later_ref, shared_ref):
@@ -75,22 +109,26 @@
         shared_ref[target, last:] = summed
 
 
-def couple_kernel(kinds_ref, parts_ref, couplings_ref, coupled_ref):
-    width = couplings_ref.shape[1]
+def couple_kernel(parts_ref, matrices_ref, coupled_ref):
+    atoms, width, _ = matrices_ref.shape
     summed = parts_ref[0].astype(jnp.float32)
     for source in range(1, parts_ref.shape[0]):
         summed = summed + parts_ref[source].astype(jnp.float32)
-    for atom in range(kinds_ref.shape[0]):
+    for atom in range(atoms):
         at = slice(atom * width, (atom + 1) * width)
         coupled_ref[at] = jnp.dot(
-            couplings_ref[kinds_ref[atom]],
+            matrices_ref[atom],
             summed[at],
             precision=lax.Precision.HIGHEST,
             preferred_element_type=jnp.float32,
         ).astype(coupled_ref.dtype)
 
 
-def backward_kernel(names_ref, earlier_ref, coupled_ref, tiles_ref, out_ref, pairs):
+def backward_kernel(
+    names_any, earlier_ref, coupled_ref, tiles_ref, out_ref, pairs, names_ref, sem
+):
+    copy = pltpu.make_async_copy(names_any, names_ref, sem)
+    copy.start()
     rows, per_row, proj, tile = tiles_ref.shape
     points = rows * tile
     groups = out_ref.shape[1] // points
@@ -101,6 +139,7 @@
         for second in range(SLOTS):
             both = jnp.concatenate([blocks[first], blocks[second]], axis=0)
             pairs[first * SLOTS + second] = both.T.astype(pairs.dtype)
+    copy.wait()
 
     def row(r, carry):
         values = tiles_ref[r].reshape(per_row * proj, tile)
@@ -133,18 +172,25 @@
     values = jnp.transpose(tiles, (0, 1, 3, 2))
 
     spread = lax.all_to_all(psi, "grid", split_axis=1, concat_axis=1, tiled=True)
-    own, edge = call(
+    own, edge, matrices = call(
         forward_kernel,
         (
             jax.ShapeDtypeStruct((BLK * proj, bands), jnp.float32),
             jax.ShapeDtypeStruct((proj, bands), jnp.bfloat16),
+            jax.ShapeDtypeStruct(species.shape + couplings.shape[1:], jnp.float32),
         ),
-        (pltpu.SMEM, pltpu.VMEM, pltpu.VMEM),
-        (pltpu.VMEM, pltpu.VMEM),
-        [pltpu.VMEM((SLOTS, proj, bands), jnp.float32)],
+        (pl.ANY, pl.ANY, pltpu.VMEM, pltpu.VMEM, pltpu.VMEM),
+        (pltpu.VMEM, pltpu.VMEM, pltpu.VMEM),
+        [
+            pltpu.VMEM((SLOTS, proj, bands), jnp.float32),
+            pltpu.VMEM((2 * AHEAD, per_row * proj, bands), jnp.float32),
+            pltpu.SMEM(names.shape, jnp.int32),
+            pltpu.SMEM(species.shape, jnp.int32),
+            pltpu.SemaphoreType.DMA((2,)),
+        ],
         flops,
         moved,
-    )(names, spread, values)
+    )(names, species, spread, values, couplings)
     later = from_behind(edge, "band", -1)
     shared = call(
         share_kernel,
@@ -156,16 +202,20 @@
     coupled = call(
         couple_kernel,
         jax.ShapeDtypeStruct((BLK * proj, bands), jnp.bfloat16),
-        (pltpu.SMEM, pltpu.VMEM, pltpu.VMEM),
+        (pltpu.VMEM, pltpu.VMEM),
         pltpu.VMEM,
-    )(species, parts, couplings)
+    )(parts, matrices)
     earlier = from_behind(coupled[last:], "band", 1)
     result = call(
         backward_kernel,
         jax.ShapeDtypeStruct(psi.shape, jnp.bfloat16),
-        (pltpu.SMEM, pltpu.VMEM, pltpu.VMEM, pltpu.VMEM),
+        (pl.ANY, pltpu.VMEM, pltpu.VMEM, pltpu.VMEM),
         pltpu.VMEM,
-        [pltpu.VMEM((SLOTS * SLOTS, bands, per_row * proj), jnp.bfloat16)],
+        [
+            pltpu.VMEM((SLOTS * SLOTS, bands, per_row * proj), jnp.bfloat16),
+            pltpu.SMEM(names.shape, jnp.int32),
+            pltpu.SemaphoreType.DMA(()),
+        ],
         flops,
         moved,
     )(names, earlier, coupled, values)

time: 117 us -> 116 us (level)
  no operation moved by 1% of the time
where the time goes in v5:
time: 116 us
  blocking collectives  99.2 us (86%)
  starting transfers between devices  5.55 us (5%)
  waiting for transfers between devices  5.04 us (4%)
  Pallas kernels  4.16 us (4%)
  local copies, waits for them, and re-layouts  1.68 us (1%)
    all_to_all x1, blocking collectives, body(): lax.all_to_all(psi, 'grid', split_axis=1, concat_axis=1, tiled=True)  45.6 us
    all_to_all x1, blocking collectives, body(): lax.all_to_all(result, 'grid', split_axis=1, concat_axis=1, tiled=True)  41 us
    all_to_all x1, blocking collectives, body(): lax.all_to_all(shared, 'grid', split_axis=0, concat_axis=0, tiled=True)  12.5 us
    ppermute x2, starting transfers between devices, from_behind(): lax.ppermute(block, axis, [(i, (i + distance) % size) for i in range(size)])  5.55 us
    ppermute x2, waiting for transfers between devices, from_behind(): lax.ppermute(block, axis, [(i, (i + distance) % size) for i in range(size)])  5.04 us
    pallas_call x1, Pallas kernels, body(): call(forward_kernel, (jax.ShapeDtypeStruct((BLK * proj, bands), jnp.float...  2.32 us
  transfers between devices with their start and end apart: 2, of which 2 were waited for; matrix products, arithmetic and copies ran while one was open for 0% of the time, Pallas kernels for 0%

profile of v5, /device:TPU:97, one launch (start us, length us, event | category | flops | bytes accessed | tf_op | source)
XLA Modules:
  0.0 115.7 jit_solution(9504040277840051611)
XLA Ops:
  0.0 0.0 copy-start
  0.0 0.0 copy-start.1
  0.0 0.0 copy-start.2
  0.0 0.0 copy-start.3
  0.0 45.6 %all_to_all.28 = bf16[8,16,12288]{2,0,1:T(8,128)(2,1)S(1)} all-to-all(bf16[8,16,12288]{2,0,1:T(8,128)(2,1)} %bitcast.13), channel_id=1, replica_groups=mesh['band'=16,'grid'=16] {'grid'}, dimensions={1} | all-to-all | bytes 6291456 | tf_op jit(solution)/shard_map/all_to_all | solution.py:174
  45.6 0.0 copy-done
  45.6 0.0 copy-done.1
  45.7 0.0 copy-done.2
  45.7 0.0 copy-done.3
  45.7 2.3 %shard_map.55 = (f32[128,128]{1,0:T(8,128)S(1)}, bf16[64,128]{1,0:T(8,128)(2,1)S(1)}, f32[8,16,16]{2,1,0:T(8,128)S(1)}) custom-call(s32[2,96]{1,0:T(2,128)S(1)} %bitcast.10, s32[8]{0:T(128)S(1)} %copy-done.3, bf16[8,196608]{1,0:T(8,128)(2,1)S(1)} %bitcast.6, bf16[96,2,64,128]{3,2,1,0:T(8,128)(2,1)S(1)} %bitcast.8, f32[2,16,16]{2,1,0:T(8,128)S(1)} %copy-done.1), custom_call_target="tpu_custom_call" | custom-call | flops 402653184 | bytes 6291456 | tf_op jit(solution)/shard_map/pallas_call | solution.py:175
  48.0 2.0 %collective-permute-start = (bf16[64,128]{1,0:T(8,128)(2,1)S(1)}, bf16[64,128]{1,0:T(8,128)(2,1)S(1)}, u32[]{:S(2)}, u32[]{:S(2)}) collective-permute-start(bf16[64,128]{1,0:T(8,128)(2,1)S(1)} %get-tuple-element.9), channel_id=1, source_target_pairs={{0,240},{16,0},{32,16},{48,32},{64,48},{80,64},{96,80},{112,96},{1... | collective-permute-start | bytes 49160 | tf_op jit(solution)/shard_map/ppermute | solution.py:159
  50.0 4.2 %collective-permute-done.later_ref = bf16[64,128]{1,0:T(8,128)(2,1)S(1)} collective-permute-done((bf16[64,128]{1,0:T(8,128)(2,1)S(1)}, bf16[64,128]{1,0:T(8,128)(2,1)S(1)}, u32[]{:S(2)}, u32[]{:S(2)}) %collective-permute-start) | collective-permute-done | bytes 16416 | tf_op jit(solution)/shard_map/ppermute | solution.py:159
  54.2 12.5 %all_to_all.29.parts_ref = bf16[16,128,128]{2,1,0:T(8,128)(2,1)S(1)} all-to-all(bf16[16,128,128]{2,1,0:T(8,128)(2,1)S(1)} %shard_map.56), channel_id=1, replica_groups=mesh['band'=16,'grid'=16] {'grid'}, dimensions={0} | all-to-all | bytes 1048576 | tf_op jit(solution)/shard_map/all_to_all | solution.py:201
  66.7 0.2 shard_map.57.coupled_ref
  67.0 3.6 %collective-permute-start.1 = (bf16[64,128]{1,0:T(8,128)(2,1)S(1)}, bf16[64,128]{1,0:T(8,128)(2,1)S(1)}, u32[]{:S(2)}, u32[]{:S(2)}) collective-permute-start(bf16[64,128]{1,0:T(8,128)(2,1)S(1)} %slice.4), channel_id=1, source_target_pairs={{0,16},{16,32},{32,48},{48,64},{64,80},{80,96},{96,112},{112,128},... | collective-permute-start | bytes 49160 | tf_op jit(solution)/shard_map/ppermute | solution.py:159
  70.5 0.9 collective-permute-done.1.earlier_ref
  71.4 1.5 %shard_map.58 = bf16[8,196608]{1,0:T(8,128)(2,1)S(1)} custom-call(s32[2,96]{1,0:T(2,128)S(1)} %bitcast.11, bf16[64,128]{1,0:T(8,128)(2,1)S(1)} %collective-permute-done.1.earlier_ref, bf16[128,128]{1,0:T(8,128)(2,1)S(1)} %shard_map.57.coupled_ref, bf16[96,2,64,128]{3,2,1,0:T(8,128)(2,1)S(1)} %bitcast.9), custom_call_target="tpu_custom_call" | custom-call | flops 402653184 | bytes 6291456 | tf_op jit(solution)/shard_map/pallas_call | solution.py:209
  72.9 41.0 %all_to_all.30 = bf16[8,16,12288]{2,0,1:T(8,128)(2,1)S(1)} all-to-all(bf16[8,16,12288]{2,0,1:T(8,128)(2,1)S(1)} %bitcast.7), channel_id=1, replica_groups=mesh['band'=16,'grid'=16] {'grid'}, dimensions={1} | all-to-all | bytes 6291456 | tf_op jit(solution)/shard_map/all_to_all | solution.py:222
  114.0 1.7 %copy.7 = bf16[8,196608]{1,0:T(8,128)(2,1)} copy(bf16[8,196608]{1,0:T(8,128)(2,1)S(1)} %bitcast.12) | data formatting | bytes 6291456
  (2 shorter events, 0.0 us)
Async XLA Ops:
  0.0 45.6 %copy-start = (bf16[96,2,128,64]{2,3,1,0:T(8,128)(2,1)S(1)}, bf16[96,2,128,64]{2,3,1,0:T(8,128)(2,1)}, u32[]{:S(2)}) copy-start(bf16[96,2,128,64]{2,3,1,0:T(8,128)(2,1)} %param.6) | copy-start | bytes 9437188
  0.0 45.6 %copy-start.1 = (f32[2,16,16]{2,1,0:T(8,128)S(1)}, f32[2,16,16]{2,1,0:T(8,128)}, u32[]{:S(2)}) copy-start(f32[2,16,16]{2,1,0:T(8,128)} %couplings_ref.1) | copy-start | bytes 6148
  0.0 45.6 %copy-start.2 = (s32[96,2]{0,1:T(2,128)S(1)}, s32[96,2]{0,1:T(2,128)}, u32[]{:S(2)}) copy-start(s32[96,2]{0,1:T(2,128)} %param.7) | copy-start | bytes 2308
  0.0 45.7 %copy-start.3 = (s32[8]{0:T(128)S(1)}, s32[8]{0:T(128)}, u32[]{:S(2)}) copy-start(s32[8]{0:T(128)} %kinds_any.1) | copy-start | bytes 100
  48.0 6.1 %collective-permute-start = (bf16[64,128]{1,0:T(8,128)(2,1)S(1)}, bf16[64,128]{1,0:T(8,128)(2,1)S(1)}, u32[]{:S(2)}, u32[]{:S(2)}) collective-permute-start(bf16[64,128]{1,0:T(8,128)(2,1)S(1)} %get-tuple-element.9), channel_id=1, source_target_pairs={{0,240},{16,0},{32,16},{48,32},{64,48},{80,64},{96,80},{112,96},{1... | collective-permute-start | bytes 49160 | tf_op jit(solution)/shard_map/ppermute | solution.py:159
  67.0 4.4 %collective-permute-start.1 = (bf16[64,128]{1,0:T(8,128)(2,1)S(1)}, bf16[64,128]{1,0:T(8,128)(2,1)S(1)}, u32[]{:S(2)}, u32[]{:S(2)}) collective-permute-start(bf16[64,128]{1,0:T(8,128)(2,1)S(1)} %slice.4), channel_id=1, source_target_pairs={{0,16},{16,32},{32,48},{48,64},{64,80},{80,96},{96,112},{112,128},... | collective-permute-start | bytes 49160 | tf_op jit(solution)/shard_map/ppermute | solution.py:159

commit v6 on v5

--- a/solution.py
+++ b/solution.py
@@ -1,3 +1,5 @@
+import functools
+
 import jax
 import jax.numpy as jnp
 from jax import lax
@@ -125,7 +127,7 @@
 
 
 def backward_kernel(
-    names_any, earlier_ref, coupled_ref, tiles_ref, out_ref, pairs, names_ref, sem
+    order, names_any, earlier_ref, coupled_ref, tiles_ref, out_ref, pairs, names_ref, sem
 ):
     copy = pltpu.make_async_copy(names_any, names_ref, sem)
     copy.start()
@@ -147,11 +149,27 @@
         result = jnp.dot(chosen, values, preferred_element_type=jnp.float32)
         result = result.astype(out_ref.dtype)
         for g in range(groups):
-            at = pl.ds(pl.multiple_of(g * points + r * tile, tile), tile)
+            at = pl.ds(pl.multiple_of(order.index(g) * points + r * tile, tile), tile)
             out_ref[:, at] = result[g * local : (g + 1) * local]
         return carry
 
     lax.fori_loop(0, rows, row, 0, unroll=rows)
+
+
+def place_kernel(order, blocks_ref, out_any, sems):
+    width = blocks_ref.shape[1] // len(order)
+    copies = [
+        pltpu.make_async_copy(
+            blocks_ref.at[:, pl.ds(k * width, width)],
+            out_any.at[:, pl.ds(device * width, width)],
+            sems.at[k],
+        )
+        for k, device in enumerate(order)
+    ]
+    for copy in copies:
+        copy.start()
+    for copy in copies:
+        copy.wait()
 
 
 def from_behind(block, axis, distance):
@@ -169,6 +187,7 @@
     moved = 2 * (bands * points + tiles.size)
     last = (BLK - EDGE) * proj
     names = tile_block.T
+    order = [i ^ (i >> 1) for i in range(splits)]
     values = jnp.transpose(tiles, (0, 1, 3, 2))
 
     spread = lax.all_to_all(psi, "grid", split_axis=1, concat_axis=1, tiled=True)
@@ -207,7 +226,7 @@
     )(parts, matrices)
     earlier = from_behind(coupled[last:], "band", 1)
     result = call(
-        backward_kernel,
+        functools.partial(backward_kernel, order),
         jax.ShapeDtypeStruct(psi.shape, jnp.bfloat16),
         (pl.ANY, pltpu.VMEM, pltpu.VMEM, pltpu.VMEM),
         pltpu.VMEM,
@@ -219,7 +238,16 @@
         flops,
         moved,
     )(names, earlier, coupled, values)
-    return lax.all_to_all(result, "grid", split_axis=1, concat_axis=1, tiled=True)
+    returned = lax.all_to_all(
+        result, "grid", split_axis=1, concat_axis=1, tiled=True, axis_index_groups=[order]
+    )
+    return call(
+        functools.partial(place_kernel, order),
+        jax.ShapeDtypeStruct(psi.shape, jnp.bfloat16),
+        (pltpu.VMEM,),
+        pl.ANY,
+        [pltpu.SemaphoreType.DMA((splits,))],
+    )(returned)
 
 
 def solution(mesh):

time: 116 us -> 115 us (level)
  Pallas kernels: 4.16 us -> 5.94 us
  local copies, waits for them, and re-layouts: 1.68 us -> 0.02 us
    pallas_call x1 -> x2, Pallas kernels: 1.55 us -> 3.33 us  [the longest x1 1.78 us: body(): call(functools.partial(place_kernel, order), jax.ShapeDtypeStruct(psi.sha...]
    unnamed x9 -> x8, local copies, waits for them, and re-layouts: 1.68 us -> 0.02 us
where the time goes in v6:
time: 115 us
  blocking collectives  98.1 us (85%)
  Pallas kernels  5.94 us (5%)
  starting transfers between devices  5.57 us (5%)
  waiting for transfers between devices  5 us (4%)
    all_to_all x1, blocking collectives, body(): lax.all_to_all(psi, 'grid', split_axis=1, concat_axis=1, tiled=True)  45.6 us
    all_to_all x1, blocking collectives, body(): lax.all_to_all(result, 'grid', split_axis=1, concat_axis=1, tiled=True, a...  40 us
    all_to_all x1, blocking collectives, body(): lax.all_to_all(shared, 'grid', split_axis=0, concat_axis=0, tiled=True)  12.5 us
    ppermute x2, starting transfers between devices, from_behind(): lax.ppermute(block, axis, [(i, (i + distance) % size) for i in range(size)])  5.57 us
    ppermute x2, waiting for transfers between devices, from_behind(): lax.ppermute(block, axis, [(i, (i + distance) % size) for i in range(size)])  5 us
    pallas_call x1, Pallas kernels, body(): call(forward_kernel, (jax.ShapeDtypeStruct((BLK * proj, bands), jnp.float...  2.32 us
  transfers between devices with their start and end apart: 2, of which 2 were waited for; matrix products, arithmetic and copies ran while one was open for 0% of the time, Pallas kernels for 0%

profile of v6, /device:TPU:97, one launch (start us, length us, event | category | flops | bytes accessed | tf_op | source)
XLA Modules:
  0.0 114.7 jit_solution(15875704829751311526)
XLA Ops:
  0.0 0.0 copy-start
  0.0 0.0 copy-start.1
  0.0 0.0 copy-start.2
  0.0 0.0 copy-start.3
  0.0 45.6 %all_to_all.27 = bf16[8,16,12288]{2,0,1:T(8,128)(2,1)S(1)} all-to-all(bf16[8,16,12288]{2,0,1:T(8,128)(2,1)} %bitcast.13), channel_id=1, replica_groups=mesh['band'=16,'grid'=16] {'grid'}, dimensions={1} | all-to-all | bytes 6291456 | tf_op jit(solution)/shard_map/all_to_all | solution.py:193
  45.6 0.0 copy-done
  45.6 0.0 copy-done.1
  45.7 0.0 copy-done.2
  45.7 0.0 copy-done.3
  45.7 2.3 %shard_map.55 = (f32[128,128]{1,0:T(8,128)S(1)}, bf16[64,128]{1,0:T(8,128)(2,1)S(1)}, f32[8,16,16]{2,1,0:T(8,128)S(1)}) custom-call(s32[2,96]{1,0:T(2,128)S(1)} %bitcast.11, s32[8]{0:T(128)S(1)} %copy-done.3, bf16[8,196608]{1,0:T(8,128)(2,1)S(1)} %bitcast.7, bf16[96,2,64,128]{3,2,1,0:T(8,128)(2,1)S(1)} %bitcast.9, f32[2,16,16]{2,1,0:T(8,128)S(1)} %copy-done.1), custom_call_target="tpu_custom_call" | custom-call | flops 402653184 | bytes 6291456 | tf_op jit(solution)/shard_map/pallas_call | solution.py:194
  48.0 2.0 %collective-permute-start = (bf16[64,128]{1,0:T(8,128)(2,1)S(1)}, bf16[64,128]{1,0:T(8,128)(2,1)S(1)}, u32[]{:S(2)}, u32[]{:S(2)}) collective-permute-start(bf16[64,128]{1,0:T(8,128)(2,1)S(1)} %get-tuple-element.9), channel_id=1, source_target_pairs={{0,240},{16,0},{32,16},{48,32},{64,48},{80,64},{96,80},{112,96},{1... | collective-permute-start | bytes 49160 | tf_op jit(solution)/shard_map/ppermute | solution.py:177
  50.0 4.1 %collective-permute-done.later_ref = bf16[64,128]{1,0:T(8,128)(2,1)S(1)} collective-permute-done((bf16[64,128]{1,0:T(8,128)(2,1)S(1)}, bf16[64,128]{1,0:T(8,128)(2,1)S(1)}, u32[]{:S(2)}, u32[]{:S(2)}) %collective-permute-start) | collective-permute-done | bytes 16416 | tf_op jit(solution)/shard_map/ppermute | solution.py:177
  54.2 12.5 %all_to_all.28.parts_ref = bf16[16,128,128]{2,1,0:T(8,128)(2,1)S(1)} all-to-all(bf16[16,128,128]{2,1,0:T(8,128)(2,1)S(1)} %shard_map.56), channel_id=1, replica_groups=mesh['band'=16,'grid'=16] {'grid'}, dimensions={0} | all-to-all | bytes 1048576 | tf_op jit(solution)/shard_map/all_to_all | solution.py:220
  66.7 0.2 shard_map.57.coupled_ref
  66.9 3.6 %collective-permute-start.1 = (bf16[64,128]{1,0:T(8,128)(2,1)S(1)}, bf16[64,128]{1,0:T(8,128)(2,1)S(1)}, u32[]{:S(2)}, u32[]{:S(2)}) collective-permute-start(bf16[64,128]{1,0:T(8,128)(2,1)S(1)} %slice.4), channel_id=1, source_target_pairs={{0,16},{16,32},{32,48},{48,64},{64,80},{80,96},{96,112},{112,128},... | collective-permute-start | bytes 49160 | tf_op jit(solution)/shard_map/ppermute | solution.py:177
  70.5 0.9 collective-permute-done.1.earlier_ref
  71.4 1.5 %shard_map.58 = bf16[8,196608]{1,0:T(8,128)(2,1)S(1)} custom-call(s32[2,96]{1,0:T(2,128)S(1)} %bitcast.12, bf16[64,128]{1,0:T(8,128)(2,1)S(1)} %collective-permute-done.1.earlier_ref, bf16[128,128]{1,0:T(8,128)(2,1)S(1)} %shard_map.57.coupled_ref, bf16[96,2,64,128]{3,2,1,0:T(8,128)(2,1)S(1)} %bitcast.10), custom_call_target="tpu_custom_call" | custom-call | flops 402653184 | bytes 6291456 | tf_op jit(solution)/shard_map/pallas_call | solution.py:228
  72.9 40.0 %all_to_all.29 = bf16[8,16,12288]{2,0,1:T(8,128)(2,1)S(1)} all-to-all(bf16[8,16,12288]{2,0,1:T(8,128)(2,1)S(1)} %bitcast.8), channel_id=1, replica_groups={{0,1,3,2,6,7,5,4,12,13,15,14,10,11,9,8},{16,17,19,18,22,23,21,20,28,29,..., dimensions={1} | all-to-all | bytes 6291456 | tf_op jit(solution)/shard_map/all_to_all | solution.py:241
  112.9 1.8 %shard_map.59 = bf16[8,196608]{1,0:T(8,128)(2,1)} custom-call(bf16[8,196608]{1,0:T(8,128)(2,1)S(1)} %bitcast.6), custom_call_target="tpu_custom_call" | custom-call | tf_op jit(solution)/shard_map/pallas_call | solution.py:244
  (2 shorter events, 0.0 us)
Async XLA Ops:
  0.0 45.6 %copy-start = (bf16[96,2,128,64]{2,3,1,0:T(8,128)(2,1)S(1)}, bf16[96,2,128,64]{2,3,1,0:T(8,128)(2,1)}, u32[]{:S(2)}) copy-start(bf16[96,2,128,64]{2,3,1,0:T(8,128)(2,1)} %param.6) | copy-start | bytes 9437188
  0.0 45.6 %copy-start.1 = (f32[2,16,16]{2,1,0:T(8,128)S(1)}, f32[2,16,16]{2,1,0:T(8,128)}, u32[]{:S(2)}) copy-start(f32[2,16,16]{2,1,0:T(8,128)} %couplings_ref.1) | copy-start | bytes 6148
  0.0 45.6 %copy-start.2 = (s32[96,2]{0,1:T(2,128)S(1)}, s32[96,2]{0,1:T(2,128)}, u32[]{:S(2)}) copy-start(s32[96,2]{0,1:T(2,128)} %param.7) | copy-start | bytes 2308
  0.0 45.7 %copy-start.3 = (s32[8]{0:T(128)S(1)}, s32[8]{0:T(128)}, u32[]{:S(2)}) copy-start(s32[8]{0:T(128)} %kinds_any.1) | copy-start | bytes 100
  48.0 6.1 %collective-permute-start = (bf16[64,128]{1,0:T(8,128)(2,1)S(1)}, bf16[64,128]{1,0:T(8,128)(2,1)S(1)}, u32[]{:S(2)}, u32[]{:S(2)}) collective-permute-start(bf16[64,128]{1,0:T(8,128)(2,1)S(1)} %get-tuple-element.9), channel_id=1, source_target_pairs={{0,240},{16,0},{32,16},{48,32},{64,48},{80,64},{96,80},{112,96},{1... | collective-permute-start | bytes 49160 | tf_op jit(solution)/shard_map/ppermute | solution.py:177
  66.9 4.4 %collective-permute-start.1 = (bf16[64,128]{1,0:T(8,128)(2,1)S(1)}, bf16[64,128]{1,0:T(8,128)(2,1)S(1)}, u32[]{:S(2)}, u32[]{:S(2)}) collective-permute-start(bf16[64,128]{1,0:T(8,128)(2,1)S(1)} %slice.4), channel_id=1, source_target_pairs={{0,16},{16,32},{32,48},{48,64},{64,80},{80,96},{96,112},{112,128},... | collective-permute-start | bytes 49160 | tf_op jit(solution)/shard_map/ppermute | solution.py:177

commit v7 on v6

--- a/solution.py
+++ b/solution.py
@@ -10,7 +10,7 @@
 BLK = 2
 EDGE = 1
 SLOTS = BLK + EDGE
-AHEAD = 8
+AHEAD = 16
 VMEM_LIMIT = 24 * 1024 * 1024
 
 
@@ -137,10 +137,12 @@
     local = out_ref.shape[0]
     blocks = [earlier_ref[...]] + [coupled_ref[k * proj : (k + 1) * proj] for k in range(BLK)]
     blocks = [b.astype(jnp.float32) for b in blocks]
+    blocks = [jnp.concatenate([b, b], axis=0).T for b in blocks]
+    left = lax.broadcasted_iota(jnp.int32, blocks[0].shape, 1) < proj
     for first in range(SLOTS):
         for second in range(SLOTS):
-            both = jnp.concatenate([blocks[first], blocks[second]], axis=0)
-            pairs[first * SLOTS + second] = both.T.astype(pairs.dtype)
+            both = jnp.where(left, blocks[first], blocks[second])
+            pairs[first * SLOTS + second] = both.astype(pairs.dtype)
     copy.wait()
 
     def row(r, carry):
@@ -154,6 +156,11 @@
         return carry
 
     lax.fori_loop(0, rows, row, 0, unroll=rows)
+
+
+def from_behind(block, axis, distance):
+    size = lax.axis_size(axis)
+    return lax.ppermute(block, axis, [(i, (i + distance) % size) for i in range(size)])
 
 
 def place_kernel(order, blocks_ref, out_any, sems):
@@ -170,11 +177,6 @@
         copy.start()
     for copy in copies:
         copy.wait()
-
-
-def from_behind(block, axis, distance):
-    size = lax.axis_size(axis)
-    return lax.ppermute(block, axis, [(i, (i + distance) % size) for i in range(size)])
 
 
 def body(psi, tiles, tile_block, couplings, species):
@@ -188,6 +190,7 @@
     last = (BLK - EDGE) * proj
     names = tile_block.T
     order = [i ^ (i >> 1) for i in range(splits)]
+    order = order[splits // 2 :] + order[: splits // 2]
     values = jnp.transpose(tiles, (0, 1, 3, 2))
 
     spread = lax.all_to_all(psi, "grid", split_axis=1, concat_axis=1, tiled=True)

time: 115 us -> 115 us (level)
  no operation moved by 1% of the time
where the time goes in v7:
time: 115 us
  blocking collectives  98.1 us (85%)
  Pallas kernels  5.97 us (5%)
  starting transfers between devices  5.52 us (5%)
  waiting for transfers between devices  5.04 us (4%)
    all_to_all x1, blocking collectives, body(): lax.all_to_all(psi, 'grid', split_axis=1, concat_axis=1, tiled=True)  45.6 us
    all_to_all x1, blocking collectives, body(): lax.all_to_all(result, 'grid', split_axis=1, concat_axis=1, tiled=True, a...  39.9 us
    all_to_all x1, blocking collectives, body(): lax.all_to_all(shared, 'grid', split_axis=0, concat_axis=0, tiled=True)  12.5 us
    ppermute x2, starting transfers between devices, from_behind(): lax.ppermute(block, axis, [(i, (i + distance) % size) for i in range(size)])  5.52 us
    ppermute x2, waiting for transfers between devices, from_behind(): lax.ppermute(block, axis, [(i, (i + distance) % size) for i in range(size)])  5.04 us
    pallas_call x1, Pallas kernels, body(): call(forward_kernel, (jax.ShapeDtypeStruct((BLK * proj, bands), jnp.float...  2.35 us
  transfers between devices with their start and end apart: 2, of which 2 were waited for; matrix products, arithmetic and copies ran while one was open for 0% of the time, Pallas kernels for 0%

profile of v7, /device:TPU:97, one launch (start us, length us, event | category | flops | bytes accessed | tf_op | source)
XLA Modules:
  0.0 114.7 jit_solution(1699647414902407029)
XLA Ops:
  0.0 0.0 copy-start
  0.0 0.0 copy-start.1
  0.0 0.0 copy-start.2
  0.0 0.0 copy-start.3
  0.0 45.6 %all_to_all.27 = bf16[8,16,12288]{2,0,1:T(8,128)(2,1)S(1)} all-to-all(bf16[8,16,12288]{2,0,1:T(8,128)(2,1)} %bitcast.13), channel_id=1, replica_groups=mesh['band'=16,'grid'=16] {'grid'}, dimensions={1} | all-to-all | bytes 6291456 | tf_op jit(solution)/shard_map/all_to_all | solution.py:196
  45.6 0.0 copy-done
  45.6 0.0 copy-done.1
  45.7 0.0 copy-done.2
  45.7 0.0 copy-done.3
  45.7 2.4 %shard_map.55 = (f32[128,128]{1,0:T(8,128)S(1)}, bf16[64,128]{1,0:T(8,128)(2,1)S(1)}, f32[8,16,16]{2,1,0:T(8,128)S(1)}) custom-call(s32[2,96]{1,0:T(2,128)S(1)} %bitcast.11, s32[8]{0:T(128)S(1)} %copy-done.3, bf16[8,196608]{1,0:T(8,128)(2,1)S(1)} %bitcast.7, bf16[96,2,64,128]{3,2,1,0:T(8,128)(2,1)S(1)} %bitcast.9, f32[2,16,16]{2,1,0:T(8,128)S(1)} %copy-done.1), custom_call_target="tpu_custom_call" | custom-call | flops 402653184 | bytes 6291456 | tf_op jit(solution)/shard_map/pallas_call | solution.py:197
  48.0 2.0 %collective-permute-start = (bf16[64,128]{1,0:T(8,128)(2,1)S(1)}, bf16[64,128]{1,0:T(8,128)(2,1)S(1)}, u32[]{:S(2)}, u32[]{:S(2)}) collective-permute-start(bf16[64,128]{1,0:T(8,128)(2,1)S(1)} %get-tuple-element.9), channel_id=1, source_target_pairs={{0,240},{16,0},{32,16},{48,32},{64,48},{80,64},{96,80},{112,96},{1... | collective-permute-start | bytes 49160 | tf_op jit(solution)/shard_map/ppermute | solution.py:163
  50.0 4.2 %collective-permute-done.later_ref = bf16[64,128]{1,0:T(8,128)(2,1)S(1)} collective-permute-done((bf16[64,128]{1,0:T(8,128)(2,1)S(1)}, bf16[64,128]{1,0:T(8,128)(2,1)S(1)}, u32[]{:S(2)}, u32[]{:S(2)}) %collective-permute-start) | collective-permute-done | bytes 16416 | tf_op jit(solution)/shard_map/ppermute | solution.py:163
  54.2 12.5 %all_to_all.28.parts_ref = bf16[16,128,128]{2,1,0:T(8,128)(2,1)S(1)} all-to-all(bf16[16,128,128]{2,1,0:T(8,128)(2,1)S(1)} %shard_map.56), channel_id=1, replica_groups=mesh['band'=16,'grid'=16] {'grid'}, dimensions={0} | all-to-all | bytes 1048576 | tf_op jit(solution)/shard_map/all_to_all | solution.py:223
  66.7 0.2 shard_map.57.coupled_ref
  67.0 3.6 %collective-permute-start.1 = (bf16[64,128]{1,0:T(8,128)(2,1)S(1)}, bf16[64,128]{1,0:T(8,128)(2,1)S(1)}, u32[]{:S(2)}, u32[]{:S(2)}) collective-permute-start(bf16[64,128]{1,0:T(8,128)(2,1)S(1)} %slice.4), channel_id=1, source_target_pairs={{0,16},{16,32},{32,48},{48,64},{64,80},{80,96},{96,112},{112,128},... | collective-permute-start | bytes 49160 | tf_op jit(solution)/shard_map/ppermute | solution.py:163
  70.5 0.9 collective-permute-done.1.earlier_ref
  71.4 1.5 %shard_map.58 = bf16[8,196608]{1,0:T(8,128)(2,1)S(1)} custom-call(s32[2,96]{1,0:T(2,128)S(1)} %bitcast.12, bf16[64,128]{1,0:T(8,128)(2,1)S(1)} %collective-permute-done.1.earlier_ref, bf16[128,128]{1,0:T(8,128)(2,1)S(1)} %shard_map.57.coupled_ref, bf16[96,2,64,128]{3,2,1,0:T(8,128)(2,1)S(1)} %bitcast.10), custom_call_target="tpu_custom_call" | custom-call | flops 402653184 | bytes 6291456 | tf_op jit(solution)/shard_map/pallas_call | solution.py:231
  73.0 39.9 %all_to_all.29 = bf16[8,16,12288]{2,0,1:T(8,128)(2,1)S(1)} all-to-all(bf16[8,16,12288]{2,0,1:T(8,128)(2,1)S(1)} %bitcast.8), channel_id=1, replica_groups={{12,13,15,14,10,11,9,8,0,1,3,2,6,7,5,4},{28,29,31,30,26,27,25,24,16,17,..., dimensions={1} | all-to-all | bytes 6291456 | tf_op jit(solution)/shard_map/all_to_all | solution.py:244
  112.9 1.8 %shard_map.59 = bf16[8,196608]{1,0:T(8,128)(2,1)} custom-call(bf16[8,196608]{1,0:T(8,128)(2,1)S(1)} %bitcast.6), custom_call_target="tpu_custom_call" | custom-call | tf_op jit(solution)/shard_map/pallas_call | solution.py:247
  (2 shorter events, 0.0 us)
Async XLA Ops:
  0.0 45.6 %copy-start = (bf16[96,2,128,64]{2,3,1,0:T(8,128)(2,1)S(1)}, bf16[96,2,128,64]{2,3,1,0:T(8,128)(2,1)}, u32[]{:S(2)}) copy-start(bf16[96,2,128,64]{2,3,1,0:T(8,128)(2,1)} %param.6) | copy-start | bytes 9437188
  0.0 45.6 %copy-start.1 = (f32[2,16,16]{2,1,0:T(8,128)S(1)}, f32[2,16,16]{2,1,0:T(8,128)}, u32[]{:S(2)}) copy-start(f32[2,16,16]{2,1,0:T(8,128)} %couplings_ref.1) | copy-start | bytes 6148
  0.0 45.6 %copy-start.2 = (s32[96,2]{0,1:T(2,128)S(1)}, s32[96,2]{0,1:T(2,128)}, u32[]{:S(2)}) copy-start(s32[96,2]{0,1:T(2,128)} %param.7) | copy-start | bytes 2308
  0.0 45.7 %copy-start.3 = (s32[8]{0:T(128)S(1)}, s32[8]{0:T(128)}, u32[]{:S(2)}) copy-start(s32[8]{0:T(128)} %kinds_any.1) | copy-start | bytes 100
  48.0 6.1 %collective-permute-start = (bf16[64,128]{1,0:T(8,128)(2,1)S(1)}, bf16[64,128]{1,0:T(8,128)(2,1)S(1)}, u32[]{:S(2)}, u32[]{:S(2)}) collective-permute-start(bf16[64,128]{1,0:T(8,128)(2,1)S(1)} %get-tuple-element.9), channel_id=1, source_target_pairs={{0,240},{16,0},{32,16},{48,32},{64,48},{80,64},{96,80},{112,96},{1... | collective-permute-start | bytes 49160 | tf_op jit(solution)/shard_map/ppermute | solution.py:163
  67.0 4.4 %collective-permute-start.1 = (bf16[64,128]{1,0:T(8,128)(2,1)S(1)}, bf16[64,128]{1,0:T(8,128)(2,1)S(1)}, u32[]{:S(2)}, u32[]{:S(2)}) collective-permute-start(bf16[64,128]{1,0:T(8,128)(2,1)S(1)} %slice.4), channel_id=1, source_target_pairs={{0,16},{16,32},{32,48},{48,64},{64,80},{80,96},{96,112},{112,128},... | collective-permute-start | bytes 49160 | tf_op jit(solution)/shard_map/ppermute | solution.py:163

commit v8 on v6

--- a/solution.py
+++ b/solution.py
@@ -188,6 +188,7 @@
     last = (BLK - EDGE) * proj
     names = tile_block.T
     order = [i ^ (i >> 1) for i in range(splits)]
+    order = order[splits // 2 :] + order[: splits // 2]
     values = jnp.transpose(tiles, (0, 1, 3, 2))
 
     spread = lax.all_to_all(psi, "grid", split_axis=1, concat_axis=1, tiled=True)

time: 115 us -> 115 us (level)
  no operation moved by 1% of the time
where the time goes in v8:
time: 115 us
  blocking collectives  98 us (85%)
  Pallas kernels  5.93 us (5%)
  starting transfers between devices  5.56 us (5%)
  waiting for transfers between devices  5.03 us (4%)
    all_to_all x1, blocking collectives, body(): lax.all_to_all(psi, 'grid', split_axis=1, concat_axis=1, tiled=True)  45.6 us
    all_to_all x1, blocking collectives, body(): lax.all_to_all(result, 'grid', split_axis=1, concat_axis=1, tiled=True, a...  39.9 us
    all_to_all x1, blocking collectives, body(): lax.all_to_all(shared, 'grid', split_axis=0, concat_axis=0, tiled=True)  12.5 us
    ppermute x2, starting transfers between devices, from_behind(): lax.ppermute(block, axis, [(i, (i + distance) % size) for i in range(size)])  5.56 us
    ppermute x2, waiting for transfers between devices, from_behind(): lax.ppermute(block, axis, [(i, (i + distance) % size) for i in range(size)])  5.03 us
    pallas_call x1, Pallas kernels, body(): call(forward_kernel, (jax.ShapeDtypeStruct((BLK * proj, bands), jnp.float...  2.31 us
  transfers between devices with their start and end apart: 2, of which 2 were waited for; matrix products, arithmetic and copies ran while one was open for 0% of the time, Pallas kernels for 0%

profile of v8, /device:TPU:97, one launch (start us, length us, event | category | flops | bytes accessed | tf_op | source)
XLA Modules:
  0.0 114.6 jit_solution(14092929188186385516)
XLA Ops:
  0.0 0.0 copy-start
  0.0 0.0 copy-start.1
  0.0 0.0 copy-start.2
  0.0 0.0 copy-start.3
  0.0 45.6 %all_to_all.27 = bf16[8,16,12288]{2,0,1:T(8,128)(2,1)S(1)} all-to-all(bf16[8,16,12288]{2,0,1:T(8,128)(2,1)} %bitcast.13), channel_id=1, replica_groups=mesh['band'=16,'grid'=16] {'grid'}, dimensions={1} | all-to-all | bytes 6291456 | tf_op jit(solution)/shard_map/all_to_all | solution.py:194
  45.6 0.0 copy-done
  45.6 0.0 copy-done.1
  45.7 0.0 copy-done.2
  45.7 0.0 copy-done.3
  45.7 2.3 %shard_map.55 = (f32[128,128]{1,0:T(8,128)S(1)}, bf16[64,128]{1,0:T(8,128)(2,1)S(1)}, f32[8,16,16]{2,1,0:T(8,128)S(1)}) custom-call(s32[2,96]{1,0:T(2,128)S(1)} %bitcast.11, s32[8]{0:T(128)S(1)} %copy-done.3, bf16[8,196608]{1,0:T(8,128)(2,1)S(1)} %bitcast.7, bf16[96,2,64,128]{3,2,1,0:T(8,128)(2,1)S(1)} %bitcast.9, f32[2,16,16]{2,1,0:T(8,128)S(1)} %copy-done.1), custom_call_target="tpu_custom_call" | custom-call | flops 402653184 | bytes 6291456 | tf_op jit(solution)/shard_map/pallas_call | solution.py:195
  48.0 2.0 %collective-permute-start = (bf16[64,128]{1,0:T(8,128)(2,1)S(1)}, bf16[64,128]{1,0:T(8,128)(2,1)S(1)}, u32[]{:S(2)}, u32[]{:S(2)}) collective-permute-start(bf16[64,128]{1,0:T(8,128)(2,1)S(1)} %get-tuple-element.9), channel_id=1, source_target_pairs={{0,240},{16,0},{32,16},{48,32},{64,48},{80,64},{96,80},{112,96},{1... | collective-permute-start | bytes 49160 | tf_op jit(solution)/shard_map/ppermute | solution.py:177
  50.0 4.2 %collective-permute-done.later_ref = bf16[64,128]{1,0:T(8,128)(2,1)S(1)} collective-permute-done((bf16[64,128]{1,0:T(8,128)(2,1)S(1)}, bf16[64,128]{1,0:T(8,128)(2,1)S(1)}, u32[]{:S(2)}, u32[]{:S(2)}) %collective-permute-start) | collective-permute-done | bytes 16416 | tf_op jit(solution)/shard_map/ppermute | solution.py:177
  54.2 12.5 %all_to_all.28.parts_ref = bf16[16,128,128]{2,1,0:T(8,128)(2,1)S(1)} all-to-all(bf16[16,128,128]{2,1,0:T(8,128)(2,1)S(1)} %shard_map.56), channel_id=1, replica_groups=mesh['band'=16,'grid'=16] {'grid'}, dimensions={0} | all-to-all | bytes 1048576 | tf_op jit(solution)/shard_map/all_to_all | solution.py:221
  66.7 0.2 shard_map.57.coupled_ref
  66.9 3.6 %collective-permute-start.1 = (bf16[64,128]{1,0:T(8,128)(2,1)S(1)}, bf16[64,128]{1,0:T(8,128)(2,1)S(1)}, u32[]{:S(2)}, u32[]{:S(2)}) collective-permute-start(bf16[64,128]{1,0:T(8,128)(2,1)S(1)} %slice.4), channel_id=1, source_target_pairs={{0,16},{16,32},{32,48},{48,64},{64,80},{80,96},{96,112},{112,128},... | collective-permute-start | bytes 49160 | tf_op jit(solution)/shard_map/ppermute | solution.py:177
  70.5 0.9 collective-permute-done.1.earlier_ref
  71.4 1.5 %shard_map.58 = bf16[8,196608]{1,0:T(8,128)(2,1)S(1)} custom-call(s32[2,96]{1,0:T(2,128)S(1)} %bitcast.12, bf16[64,128]{1,0:T(8,128)(2,1)S(1)} %collective-permute-done.1.earlier_ref, bf16[128,128]{1,0:T(8,128)(2,1)S(1)} %shard_map.57.coupled_ref, bf16[96,2,64,128]{3,2,1,0:T(8,128)(2,1)S(1)} %bitcast.10), custom_call_target="tpu_custom_call" | custom-call | flops 402653184 | bytes 6291456 | tf_op jit(solution)/shard_map/pallas_call | solution.py:229
  72.9 39.9 %all_to_all.29 = bf16[8,16,12288]{2,0,1:T(8,128)(2,1)S(1)} all-to-all(bf16[8,16,12288]{2,0,1:T(8,128)(2,1)S(1)} %bitcast.8), channel_id=1, replica_groups={{12,13,15,14,10,11,9,8,0,1,3,2,6,7,5,4},{28,29,31,30,26,27,25,24,16,17,..., dimensions={1} | all-to-all | bytes 6291456 | tf_op jit(solution)/shard_map/all_to_all | solution.py:242
  112.8 1.8 %shard_map.59 = bf16[8,196608]{1,0:T(8,128)(2,1)} custom-call(bf16[8,196608]{1,0:T(8,128)(2,1)S(1)} %bitcast.6), custom_call_target="tpu_custom_call" | custom-call | tf_op jit(solution)/shard_map/pallas_call | solution.py:245
  (2 shorter events, 0.0 us)
Async XLA Ops:
  0.0 45.6 %copy-start = (bf16[96,2,128,64]{2,3,1,0:T(8,128)(2,1)S(1)}, bf16[96,2,128,64]{2,3,1,0:T(8,128)(2,1)}, u32[]{:S(2)}) copy-start(bf16[96,2,128,64]{2,3,1,0:T(8,128)(2,1)} %param.6) | copy-start | bytes 9437188
  0.0 45.6 %copy-start.1 = (f32[2,16,16]{2,1,0:T(8,128)S(1)}, f32[2,16,16]{2,1,0:T(8,128)}, u32[]{:S(2)}) copy-start(f32[2,16,16]{2,1,0:T(8,128)} %couplings_ref.1) | copy-start | bytes 6148
  0.0 45.6 %copy-start.2 = (s32[96,2]{0,1:T(2,128)S(1)}, s32[96,2]{0,1:T(2,128)}, u32[]{:S(2)}) copy-start(s32[96,2]{0,1:T(2,128)} %param.7) | copy-start | bytes 2308
  0.0 45.7 %copy-start.3 = (s32[8]{0:T(128)S(1)}, s32[8]{0:T(128)}, u32[]{:S(2)}) copy-start(s32[8]{0:T(128)} %kinds_any.1) | copy-start | bytes 100
  48.0 6.1 %collective-permute-start = (bf16[64,128]{1,0:T(8,128)(2,1)S(1)}, bf16[64,128]{1,0:T(8,128)(2,1)S(1)}, u32[]{:S(2)}, u32[]{:S(2)}) collective-permute-start(bf16[64,128]{1,0:T(8,128)(2,1)S(1)} %get-tuple-element.9), channel_id=1, source_target_pairs={{0,240},{16,0},{32,16},{48,32},{64,48},{80,64},{96,80},{112,96},{1... | collective-permute-start | bytes 49160 | tf_op jit(solution)/shard_map/ppermute | solution.py:177
  66.9 4.4 %collective-permute-start.1 = (bf16[64,128]{1,0:T(8,128)(2,1)S(1)}, bf16[64,128]{1,0:T(8,128)(2,1)S(1)}, u32[]{:S(2)}, u32[]{:S(2)}) collective-permute-start(bf16[64,128]{1,0:T(8,128)(2,1)S(1)} %slice.4), channel_id=1, source_target_pairs={{0,16},{16,32},{32,48},{48,64},{64,80},{80,96},{96,112},{112,128},... | collective-permute-start | bytes 49160 | tf_op jit(solution)/shard_map/ppermute | solution.py:177
